TPU v7x, 32 devices: a whole 2x2x4 slice. The times are simulated.
32 devices in a mesh: rows: 16 (over z, y, x), chan: 2 (over core).
Axes of the slice: x: 2, y: 2, z: 4, core: 2. Of those that a mesh axis runs over, the one named last changes fastest.
Arguments:
- tokens: bfloat16 [32768, 768], P('rows', 'chan'), may hold values from -6 to 6
- segments: int32 [32, 1024], P('rows'), may hold values from 0 to 7, never falling along the last dimension, each value on 1 to 512 neighbouring positions
- gain_in: float32 [768], P('chan'), may hold values from 0.5 to 1.5
- shift_in: float32 [768], P('chan'), may hold values from -1 to 1
- query_weight: bfloat16 [768, 768], P(None, 'chan'), may hold values from -0.21875 to 0.21875
- key_weight: bfloat16 [768, 768], P(None, 'chan'), may hold values from -0.21875 to 0.21875
- value_weight: bfloat16 [768, 768], P(None, 'chan'), may hold values from -0.21875 to 0.21875
- out_weight: bfloat16 [768, 768], P('chan'), may hold values from -1.75 to 1.75
- gain_mid: float32 [768], P('chan'), may hold values from 0.5 to 1.5
- shift_mid: float32 [768], P('chan'), may hold values from -1 to 1
- up_weight: bfloat16 [768, 3072], P(None, 'chan'), may hold values from -0.25259074 to 0.25259074
- down_weight: bfloat16 [3072, 768], P('chan'), may hold values from -0.109375 to 0.109375
- pair_bias: float32 [1024, 1024], replicated, may hold values from -4 to 4
- out_grad: bfloat16 [32768, 768], P('rows', 'chan'), may hold values from -6 to 6
Outputs:
- block_out: bfloat16 [32768, 768], P('rows', 'chan')
- tokens_grad: float32 [32768, 768], P('rows', 'chan')
- gain_in_grad: float32 [768], P('chan')
- shift_in_grad: float32 [768], P('chan')
- query_weight_grad: float32 [768, 768], P('rows', 'chan')
- key_weight_grad: float32 [768, 768], P('rows', 'chan')
- value_weight_grad: float32 [768, 768], P('rows', 'chan')
- out_weight_grad: float32 [768, 768], P('chan', 'rows')
- gain_mid_grad: float32 [768], P('chan')
- shift_mid_grad: float32 [768], P('chan')
- up_weight_grad: float32 [768, 3072], P('rows', 'chan')
- down_weight_grad: float32 [3072, 768], P('chan', 'rows')
- pair_bias_grad: float32 [1024, 1024], P('rows', 'chan')
Inputs may be any that keep to these rules, and one draw needn't show every extreme that they name: `segments`: segment numbers never fall along a row of 1024 tokens; no document holds more than 512 tokens.
All inputs are finite; a program needn't handle non-finite values.
Results may differ from a plain program's by a relative error of at most 0.017.
Values may be sent and summed in bfloat16 or wider, within the bound.
A program may use at most 192 MiB of HBM per device.

v0:
```python
import jax
import jax.numpy as jnp
from jax import lax
from jax.sharding import PartitionSpec as P

WIN = 256


epsilon = 1e-05


def gelu_exact(values):
    return jax.nn.gelu(values, approximate=False)


def normalize(values, gain, shift):
    feat_width = values.shape[1] * lax.axis_size("chan")
    row_total = lax.psum(jnp.sum(values, 1), "chan")
    row_mean = row_total / feat_width
    centred = values - row_mean[:, None]
    spread = lax.psum(jnp.sum(centred * centred, 1), "chan") / feat_width
    inv_scale = lax.rsqrt(spread + epsilon)[:, None]
    normed = centred * inv_scale
    norm_out = (normed * gain + shift).astype(jnp.bfloat16)
    gathered = lax.all_gather(norm_out, "chan", axis=1, tiled=True)
    return (normed, inv_scale, gathered)


def normalize_back(grad_rows, normed, inv_scale, gain):
    feat_width = grad_rows.shape[1] * lax.axis_size("chan")
    scaled = grad_rows * gain
    sum_plain, sum_normed = lax.psum((jnp.sum(scaled, 1), jnp.sum(scaled * normed, 1)), "chan")
    back_rows = inv_scale * (
        scaled - sum_plain[:, None] / feat_width - normed * (sum_normed[:, None] / feat_width)
    )
    return (back_rows, jnp.sum(grad_rows * normed, 0), jnp.sum(grad_rows, 0))


def branch_sum(partial_value):
    return lax.psum_scatter(
        partial_value.astype(jnp.bfloat16), "chan", scatter_dimension=1, tiled=True
    ).astype(jnp.float32)


def spread_grad(grad_rows):
    return lax.all_gather(grad_rows, "chan", axis=1, tiled=True)


def collect_grad(partial_value):
    return lax.psum_scatter(
        partial_value.astype(jnp.bfloat16), "chan", scatter_dimension=1, tiled=True
    ).astype(jnp.float32)


def on_device(
    tokens,
    segments,
    gain_in,
    shift_in,
    query_weight,
    key_weight,
    value_weight,
    out_weight,
    gain_mid,
    shift_mid,
    up_weight,
    down_weight,
    pair_bias,
    out_grad,
):
    seq_count, length = segments.shape
    total_rows = seq_count * length
    half_width = query_weight.shape[1]
    order_len = pair_bias.shape[0]
    offset = lax.broadcasted_iota(jnp.int32, (order_len, order_len), 0) - lax.broadcasted_iota(
        jnp.int32, (order_len, order_len), 1
    )
    inside = jnp.abs(offset) < WIN
    raised = jnp.exp(pair_bias)
    window = jnp.where(inside, raised, 1.0).astype(jnp.bfloat16)
    same_doc = segments[:, :, None] == segments[:, None, :]
    mix_weights = jnp.where(same_doc, window[None], jnp.zeros((), jnp.bfloat16))
    residual = tokens.astype(jnp.float32)
    normed_in, scale_in, full_in = normalize(residual, gain_in, shift_in)
    query_act = jnp.dot(full_in, query_weight, preferred_element_type=jnp.float32)
    key_act = jnp.dot(full_in, key_weight, preferred_element_type=jnp.float32)
    value_act = jnp.dot(full_in, value_weight, preferred_element_type=jnp.float32)
    raised_keys = jnp.exp(key_act)
    carried = jnp.concatenate(
        [(raised_keys * value_act).astype(jnp.bfloat16), raised_keys.astype(jnp.bfloat16)], 1
    )
    carried = carried.reshape(seq_count, length, 2 * half_width)
    summed = jnp.einsum("atb,abe->ate", mix_weights, carried, preferred_element_type=jnp.float32)
    summed = summed.reshape(total_rows, 2 * half_width)
    numerator = summed[:, :half_width]
    denominator = summed[:, half_width:]
    gate_act = jax.nn.sigmoid(query_act)
    mix_ratio = numerator / denominator
    mixed_out = (gate_act * mix_ratio).astype(jnp.bfloat16)
    attn_half = branch_sum(jnp.dot(mixed_out, out_weight, preferred_element_type=jnp.float32))
    middle = residual + attn_half
    normed_mid, scale_mid, full_mid = normalize(middle, gain_mid, shift_mid)
    pre_act = jnp.dot(full_mid, up_weight, preferred_element_type=jnp.float32)
    activated, act_back = jax.vjp(gelu_exact, pre_act)
    hidden = activated.astype(jnp.bfloat16)
    mlp_half = branch_sum(jnp.dot(hidden, down_weight, preferred_element_type=jnp.float32))
    block_out = (middle + mlp_half).astype(jnp.bfloat16)
    grad_full = spread_grad(out_grad)
    down_grad = jnp.dot(hidden.T, grad_full, preferred_element_type=jnp.float32)
    (pre_grad,) = act_back(jnp.dot(grad_full, down_weight.T, preferred_element_type=jnp.float32))
    pre_low = pre_grad.astype(jnp.bfloat16)
    up_grad = jnp.dot(full_mid.T, pre_low, preferred_element_type=jnp.float32)
    mid_grad = collect_grad(jnp.dot(pre_low, up_weight.T, preferred_element_type=jnp.float32))
    back_mid, gain_mid_part, shift_mid_part = normalize_back(
        mid_grad, normed_mid, scale_mid, gain_mid
    )
    middle_grad = out_grad.astype(jnp.float32) + back_mid
    attn_grad = spread_grad(middle_grad.astype(jnp.bfloat16))
    out_grad_weight = jnp.dot(mixed_out.T, attn_grad, preferred_element_type=jnp.float32)
    mixed_grad = jnp.dot(attn_grad, out_weight.T, preferred_element_type=jnp.float32)
    query_low = (mixed_grad * mix_ratio * gate_act * (1.0 - gate_act)).astype(jnp.bfloat16)
    lifted = mixed_grad * gate_act / denominator
    back_terms = jnp.concatenate(
        [lifted.astype(jnp.bfloat16), (-lifted * mix_ratio).astype(jnp.bfloat16)], 1
    )
    back_seq = back_terms.reshape(seq_count, length, 2 * half_width)
    spread_back = jnp.einsum(
        "atb,ate->abe", mix_weights, back_seq, preferred_element_type=jnp.float32
    )
    spread_back = spread_back.reshape(total_rows, 2 * half_width)
    kv_grad = spread_back[:, :half_width]
    key_low = ((spread_back[:, half_width:] + kv_grad * value_act) * raised_keys).astype(
        jnp.bfloat16
    )
    value_low = (kv_grad * raised_keys).astype(jnp.bfloat16)
    mixer_grad = jnp.einsum("ate,abe->atb", back_seq, carried, preferred_element_type=jnp.float32)
    masked_sum = jnp.sum(jnp.where(same_doc, mixer_grad, 0.0), 0)
    pair_part = jnp.where(inside, masked_sum * raised, 0.0)
    query_grad = jnp.dot(full_in.T, query_low, preferred_element_type=jnp.float32)
    key_grad = jnp.dot(full_in.T, key_low, preferred_element_type=jnp.float32)
    value_grad = jnp.dot(full_in.T, value_low, preferred_element_type=jnp.float32)
    in_partial = jnp.dot(query_low, query_weight.T, preferred_element_type=jnp.float32)
    in_partial = in_partial + jnp.dot(key_low, key_weight.T, preferred_element_type=jnp.float32)
    in_partial = in_partial + jnp.dot(value_low, value_weight.T, preferred_element_type=jnp.float32)
    in_grad = collect_grad(in_partial)
    back_in, gain_in_part, shift_in_part = normalize_back(in_grad, normed_in, scale_in, gain_in)
    tokens_grad = middle_grad + back_in
    pair_send = lax.psum_scatter(
        pair_part.astype(jnp.bfloat16), "chan", scatter_dimension=1, tiled=True
    ).astype(jnp.float32)
    query_sum, key_sum, value_sum, up_sum, pair_sum = (
        lax.psum_scatter(query_grad, "rows", scatter_dimension=0, tiled=True),
        lax.psum_scatter(key_grad, "rows", scatter_dimension=0, tiled=True),
        lax.psum_scatter(value_grad, "rows", scatter_dimension=0, tiled=True),
        lax.psum_scatter(up_grad, "rows", scatter_dimension=0, tiled=True),
        lax.psum_scatter(pair_send, "rows", scatter_dimension=0, tiled=True),
    )
    out_sum, down_sum = (
        lax.psum_scatter(out_grad_weight, "rows", scatter_dimension=1, tiled=True),
        lax.psum_scatter(down_grad, "rows", scatter_dimension=1, tiled=True),
    )
    norm_sums = lax.psum(
        jnp.stack([gain_in_part, shift_in_part, gain_mid_part, shift_mid_part]), "rows"
    )
    return (
        block_out,
        tokens_grad,
        norm_sums[0],
        norm_sums[1],
        query_sum,
        key_sum,
        value_sum,
        out_sum,
        norm_sums[2],
        norm_sums[3],
        up_sum,
        down_sum,
        pair_sum,
    )


def solution(mesh):
    placed = (
        P("rows", "chan"),
        P("rows", None),
        P("chan"),
        P("chan"),
        P(None, "chan"),
        P(None, "chan"),
        P(None, "chan"),
        P("chan", None),
        P("chan"),
        P("chan"),
        P(None, "chan"),
        P("chan", None),
        P(),
        P("rows", "chan"),
    )
    return jax.shard_map(
        on_device,
        mesh=mesh,
        in_specs=placed,
        out_specs=(
            P("rows", "chan"),
            P("rows", "chan"),
            P("chan"),
            P("chan"),
            P("rows", "chan"),
            P("rows", "chan"),
            P("rows", "chan"),
            P("chan", "rows"),
            P("chan"),
            P("chan"),
            P("rows", "chan"),
            P("chan", "rows"),
            P("rows", "chan"),
        ),
        check_vma=False,
    )
```

profile of v0, /device:TPU:0, one launch (start us, length us, event | category | flops | bytes accessed | tf_op | source)
XLA Modules:
  0.0 1204.8 jit_solution(8954249675470903453)
XLA Ops:
  24.1 10.6 all-gather.5.cloned.1.call-done
  48.3 6.0 fusion.8
  64.6 8.7 multiply_convert_fusion.5
  82.9 11.9 reduce-scatter.37.cloned.1.call-done
  111.4 12.7 %all-gather.7.cloned.1.call-done = bf16[2048,768]{1,0:T(8,128)(2,1)} async-done(((bf16[2048,384]{1,0:T(8,128)(2,1)}), bf16[2048,768]{1,0:T(8,128)(2,1)}) %all-gather.7.cloned.1.call-update) | async-done | bytes 3145744 | tf_op jit(solution)/shard_map/all_gather | solution.py:25
  124.1 33.7 %multiply_convert_fusion = (bf16[2048,1536]{1,0:T(8,128)(2,1)}, f32[2048,1536]{1,0:T(8,128)}, f32[2048,1536]{1,0:T(8,128)}) fusion(bf16[2048,768]{1,0:T(8,128)(2,1)} %all-gather.7.cloned.1.call-done, bf16[768,1536]{1,0:T(8,128)(2,1)S(1)} %copy-done), kind=kOutput, calls=%fused_computation.3 | convolution fusion | flops 5036310528 | bytes 36962304 | tf_op jit(solution)/shard_map/dot_general | solution.py:103
  157.8 16.1 %add_convert_fusion = bf16[2048,1536]{1,0:T(8,128)(2,1)S(1)} fusion(f32[2048,1536]{1,0:T(8,128)} %get-tuple-element.30, f32[2048,1536]{1,0:T(8,128)} %get-tuple-element.48, bf16[2048,768]{1,0:T(8,128)(2,1)} %all-gather.9.cloned.1.call-done, bf16[1536,768]{1,0:T(8,128)(2,1)} %param.25), kind=kOutput, calls=%fused_computation.2 | convolution fusion | flops 4875878400 | bytes 36962304 | tf_op jit(solution)/shard_map/dot_general | solution.py:110
  176.6 6.4 convolution_convert_fusion.1
  187.8 10.4 all-gather.11.cloned.1.call-start
  209.2 5.1 fusion.43
  214.4 13.4 %all-gather.11.cloned.1.call-done = bf16[2048,768]{1,0:T(8,128)(2,1)} async-done(((bf16[2048,384]{1,0:T(8,128)(2,1)}), bf16[2048,768]{1,0:T(8,128)(2,1)}) %all-gather.11.cloned.1.call-update) | async-done | bytes 3145744 | tf_op jit(solution)/shard_map/all_gather | solution.py:46
  227.8 7.7 fusion.44
  242.2 7.1 fusion.6
  251.3 9.1 convolution_convert_fusion.2
  260.4 4.8 copy.46
  265.3 6.8 fusion.7
  282.9 6.3 multiply_convert_fusion.1
  302.2 10.1 fusion.56
  312.4 10.2 fusion.55
  322.7 5.2 fusion.54
  328.0 5.4 fusion.51
  333.5 5.2 fusion.52
  338.8 5.3 fusion.53
  355.5 42.9 %psum.71 = f32[4,384]{1,0:T(4,128)S(1)} all-reduce(f32[4,384]{1,0:T(4,128)S(1)} %pad_maximum_fusion.2), channel_id=1, replica_groups=mesh['rows'=16,'chan'=2] {'rows'}, use_global_device_ids=true, to_apply=%region_24.25 | all-reduce | flops 1536 | bytes 12288 | tf_op jit(solution)/shard_map/psum | solution.py:162
  402.3 8.5 fusion.27
  410.8 48.7 %reduce-scatter.31.cloned.1.call-done = f32[1536,48]{0,1:T(8,128)} async-done(((f32[1536,768]{0,1:T(8,128)}), f32[1536,48]{0,1:T(8,128)}) %reduce-scatter.31.cloned.1.call-update) | async-done | bytes 294928 | tf_op jit(solution)/shard_map/reduce_scatter | solution.py:160
  459.5 142.1 %reduce-scatter.29.cloned.1.call-done = f32[48,1536]{1,0:T(8,128)} async-done(((f32[768,1536]{1,0:T(8,128)}), f32[48,1536]{1,0:T(8,128)}) %reduce-scatter.29.cloned.1.call-update) | async-done | bytes 294928 | tf_op jit(solution)/shard_map/reduce_scatter | solution.py:155
  601.5 128.6 %reduce-scatter.27.cloned.1.call-done = f32[384,48]{0,1:T(8,128)} async-done(((f32[384,768]{0,1:T(8,128)}), f32[384,48]{0,1:T(8,128)}) %reduce-scatter.27.cloned.1.call-update) | async-done | bytes 73744 | tf_op jit(solution)/shard_map/reduce_scatter | solution.py:159
  730.1 128.7 %reduce-scatter.21.cloned.1.call-done = f32[48,384]{1,0:T(8,128)} async-done(((f32[768,384]{1,0:T(8,128)}), f32[48,384]{1,0:T(8,128)}) %reduce-scatter.21.cloned.1.call-update) | async-done | bytes 73744 | tf_op jit(solution)/shard_map/reduce_scatter | solution.py:152
  858.8 128.5 %reduce-scatter.23.cloned.1.call-done = f32[48,384]{1,0:T(8,128)} async-done(((f32[768,384]{1,0:T(8,128)}), f32[48,384]{1,0:T(8,128)}) %reduce-scatter.23.cloned.1.call-update) | async-done | bytes 73744 | tf_op jit(solution)/shard_map/reduce_scatter | solution.py:153
  987.3 128.4 %reduce-scatter.25.cloned.1.call-done = f32[48,384]{1,0:T(8,128)} async-done(((f32[768,384]{1,0:T(8,128)}), f32[48,384]{1,0:T(8,128)}) %reduce-scatter.25.cloned.1.call-update) | async-done | bytes 73744 | tf_op jit(solution)/shard_map/reduce_scatter | solution.py:154
  1115.7 82.3 %reduce-scatter.35.cloned.1.call-done = f32[64,512]{1,0:T(8,128)} async-done(((f32[1024,512]{1,0:T(8,128)}), f32[64,512]{1,0:T(8,128)}) %reduce-scatter.35.cloned.1.call-update) | async-done | bytes 131088 | tf_op jit(solution)/shard_map/reduce_scatter | solution.py:156
  (149 shorter events, 133.4 us)
Async XLA Ops:
  7.2 117.0 %copy-start = (bf16[768,1536]{1,0:T(8,128)(2,1)S(1)}, bf16[768,1536]{1,0:T(8,128)(2,1)}, u32[]{:S(2)}) copy-start(bf16[768,1536]{1,0:T(8,128)(2,1)} %param.24) | copy-start | bytes 7077892
  7.2 9.9 copy-start.20
  7.2 9.9 copy-start.22
  7.2 27.5 %all-gather.5.cloned.1.call-start = ((), (), s32[]{:S(2)}) async-start(), calls=%async_computation.12 | async-start | bytes 4718592 | tf_op jit(solution)/shard_map/all_gather | solution.py:25
  11.8 8.2 copy-start.15
  20.0 14.7 %copy-start.13 = (bf16[768,384]{1,0:T(8,128)(2,1)S(1)}, bf16[768,384]{1,0:T(8,128)(2,1)}, u32[]{:S(2)}) copy-start(bf16[768,384]{1,0:T(8,128)(2,1)} %param.20) | copy-start | bytes 1769476
  20.0 74.8 %reduce-scatter.37.cloned.1.call-start = ((), (), s32[]{:S(2)}) async-start(), calls=%async_computation.24 | async-start | bytes 4718592
  24.1 14.1 %copy-start.9 = (bf16[768,384]{1,0:T(8,128)(2,1)S(1)}, bf16[768,384]{1,0:T(8,128)(2,1)}, u32[]{:S(2)}) copy-start(bf16[768,384]{1,0:T(8,128)(2,1)} %param.19) | copy-start | bytes 1769476
  64.6 9.8 copy-start.24
  82.6 41.5 %all-gather.7.cloned.1.call-start = ((), (), s32[]{:S(2)}) async-start(), calls=%async_computation.13 | async-start | bytes 4718592 | tf_op jit(solution)/shard_map/all_gather | solution.py:25
  97.4 10.1 copy-start.19
  97.4 10.1 copy-start.23
  110.8 47.0 %all-gather.9.cloned.1.call-start = ((), (), s32[]{:S(2)}) async-start(), calls=%async_computation.14 | async-start | bytes 4718592 | tf_op jit(solution)/shard_map/all_gather | solution.py:46
  111.4 88.6 %reduce-scatter.41.cloned.1.call-start = ((), (), s32[]{:S(2)}) async-start(), calls=%async_computation.26 | async-start | bytes 4718592
  187.7 14.8 %copy-start.2 = (bf16[2048,384]{1,0:T(8,128)(2,1)S(1)}, bf16[2048,384]{1,0:T(8,128)(2,1)}, u32[]{:S(2)}) copy-start(bf16[2048,384]{1,0:T(8,128)(2,1)} %param.14) | copy-start | bytes 4718596
  187.8 40.0 %all-gather.11.cloned.1.call-start = ((), (), s32[]{:S(2)}) async-start(), calls=%async_computation.15 | async-start | bytes 4718592 | tf_op jit(solution)/shard_map/all_gather | solution.py:46
  209.2 18.6 %copy-start.25 = (bf16[384,768]{1,0:T(8,128)(2,1)S(1)}, bf16[384,768]{1,0:T(8,128)(2,1)}, u32[]{:S(2)}) copy-start(bf16[384,768]{1,0:T(8,128)(2,1)} %param.21) | copy-start | bytes 1769476
  214.3 129.9 %reduce-scatter.33.cloned.1.call-start = ((), (), s32[]{:S(2)}) async-start(), calls=%async_computation.22 | async-start | bytes 3145728 | tf_op jit(solution)/shard_map/reduce_scatter | solution.py:148
  242.2 7.1 copy-start.3
  251.3 95.8 %reduce-scatter.39.cloned.1.call-start = ((), (), s32[]{:S(2)}) async-start(), calls=%async_computation.25 | async-start | bytes 4718592
  265.2 84.6 %reduce-scatter.43.cloned.1.call-start = ((), (), s32[]{:S(2)}) async-start(), calls=%async_computation.27 | async-start | bytes 4718592
  282.9 6.3 copy-start.10
  302.2 157.3 %reduce-scatter.31.cloned.1.call-start = ((), (), s32[]{:S(2)}) async-start(), calls=%async_computation.21 | async-start | bytes 5013504 | tf_op jit(solution)/shard_map/reduce_scatter | solution.py:160
  312.3 289.2 %reduce-scatter.29.cloned.1.call-start = ((), (), s32[]{:S(2)}) async-start(), calls=%async_computation.20 | async-start | bytes 5013504 | tf_op jit(solution)/shard_map/reduce_scatter | solution.py:155
  322.6 407.5 %reduce-scatter.27.cloned.1.call-start = ((), (), s32[]{:S(2)}) async-start(), calls=%async_computation.19 | async-start | bytes 1253376 | tf_op jit(solution)/shard_map/reduce_scatter | solution.py:159
  327.9 530.8 %reduce-scatter.21.cloned.1.call-start = ((), (), s32[]{:S(2)}) async-start(), calls=%async_computation.16 | async-start | bytes 1253376 | tf_op jit(solution)/shard_map/reduce_scatter | solution.py:152
  333.4 653.9 %reduce-scatter.23.cloned.1.call-start = ((), (), s32[]{:S(2)}) async-start(), calls=%async_computation.17 | async-start | bytes 1253376 | tf_op jit(solution)/shard_map/reduce_scatter | solution.py:153
  338.7 777.0 %reduce-scatter.25.cloned.1.call-start = ((), (), s32[]{:S(2)}) async-start(), calls=%async_computation.18 | async-start | bytes 1253376 | tf_op jit(solution)/shard_map/reduce_scatter | solution.py:154
  344.1 854.0 %reduce-scatter.35.cloned.1.call-start = ((), (), s32[]{:S(2)}) async-start(), calls=%async_computation.23 | async-start | bytes 2228224 | tf_op jit(solution)/shard_map/reduce_scatter | solution.py:156
  347.1 5.3 copy-start.16
  347.1 5.3 copy-start.18
  402.3 795.8 %copy-start.1 = (bf16[768,1536]{1,0:T(8,128)(2,1)S(1)}, bf16[768,1536]{1,0:T(8,128)(2,1)}, u32[]{:S(2)}) copy-start(bf16[768,1536]{1,0:T(8,128)(2,1)} %param.24) | copy-start | bytes 7077892
  (14 other events, 43.0 us)
Sparse Core Ops, SparseCore 0:
  20.1 14.5 all-gather.4
  82.7 12.0 reduce-scatter.36
  110.9 13.1 all-gather.6
  125.6 13.1 all-gather.8
  187.9 12.0 reduce-scatter.40
  214.4 13.2 all-gather.10
  251.4 10.7 reduce-scatter.32
  265.3 12.0 reduce-scatter.38
  302.3 12.0 reduce-scatter.42
  320.8 138.5 reduce-scatter.30
  465.2 136.2 reduce-scatter.28
  607.4 122.6 reduce-scatter.26
  736.2 122.5 reduce-scatter.20
  864.7 122.5 reduce-scatter.22
  993.2 122.5 reduce-scatter.24
  1118.5 79.4 reduce-scatter.34
where the time goes:
time: 1220 us; the launch traced here: 1200 us
  waiting for transfers between devices  839 us (69%)
  matrix products  161 us (13%)
  local copies, waits for them, and re-layouts  65.7 us (5%)
  blocking collectives  59.7 us (5%)
  other arithmetic  54.4 us (4%)
  between operations  14.5 us (1%)
    reduce_scatter x1, waiting for transfers between devices, on_device(): lax.psum_scatter(up_grad, 'rows', scatter_dimension=0, tiled=True)  142 us
    reduce_scatter x1, waiting for transfers between devices, on_device(): lax.psum_scatter(query_grad, 'rows', scatter_dimension=0, tiled=True)  129 us
    reduce_scatter x1, waiting for transfers between devices, on_device(): lax.psum_scatter(out_grad_weight, 'rows', scatter_dimension=1, tiled=True)  129 us
    reduce_scatter x1, waiting for transfers between devices, on_device(): lax.psum_scatter(key_grad, 'rows', scatter_dimension=0, tiled=True)  129 us
    reduce_scatter x1, waiting for transfers between devices, on_device(): lax.psum_scatter(value_grad, 'rows', scatter_dimension=0, tiled=True)  128 us
    reduce_scatter x1, waiting for transfers between devices, on_device(): lax.psum_scatter(pair_send, 'rows', scatter_dimension=0, tiled=True)  82.3 us
    unnamed x72, local copies, waits for them, and re-layouts  49.4 us
    reduce_scatter x1, waiting for transfers between devices, on_device(): lax.psum_scatter(down_grad, 'rows', scatter_dimension=1, tiled=True)  48.7 us
  transfers between devices with their start and end apart: 16, of which 12 were waited for; matrix products, arithmetic and copies ran while one was open for 12% of the time, Pallas kernels for 0%

commit v1 on v0

v1 whole, which is shorter than its diff:
```python
import functools

import jax
import jax.numpy as jnp
from jax import lax
from jax.experimental import pallas as pl
from jax.experimental.pallas import tpu as pltpu
from jax.sharding import PartitionSpec as P

MESH = pl.DeviceIdType.MESH
WIN = 256
EPSILON = 1e-05
TILE = 128
COLS = 256
SLOTS = 4
f32 = jnp.float32
bf16 = jnp.bfloat16


def dot(left, right, cl=1, cr=0):
    return lax.dot_general(left, right, (((cl,), (cr,)), ((), ())), preferred_element_type=f32)


def dot_nt(left, right):
    return dot(left, right, 1, 1)


def dot_tn(left, right):
    return dot(left, right, 0, 0)


def gelu_pair(p):
    phi = 0.5 * (1.0 + lax.erf(p * 0.7071067811865476))
    return p * phi, phi + p * (jnp.exp(-0.5 * p * p) * 0.3989422804014327)


def fold_rows(v):
    return jnp.sum(v.reshape(v.shape[0] // 8, 8, v.shape[1]), axis=0)


def block_kernel(T, D, FH, R, fused, names, *all_refs):
    ref = dict(zip(names, all_refs))
    half = D // 2
    blocks = FH // COLS
    nb = R if fused else 16
    nz = nb // 4
    sh, sp = D // nb, T // nb
    r = lax.axis_index("rows")
    c = lax.axis_index("chan")
    o = 1 - c
    mx, my, mz = lax.rem(r, 2), lax.rem(r // 2, 2), r // 4
    dev_c = (r, o)
    dev_x = (r + 1 - 2 * mx, c)
    dev_y = (r + 2 - 4 * my, c)
    dev_z = [(lax.rem(mz + j, nz) * 4 + lax.rem(r, 4), c) for j in range(1, nz)]
    own_half = pl.ds(pl.multiple_of(c * half, TILE), half)
    other_half = pl.ds(pl.multiple_of(o * half, TILE), half)

    XB, OG, HN, G = ref["XB"], ref["OG"], ref["HN"], ref["G"]
    Y, QQ, RT, RZ, T2 = ref["Y"], ref["QQ"], ref["RT"], ref["RZ"], ref["T2"]
    AB, MM, F1, F3, ST = ref["AB"], ref["MM"], ref["F1"], ref["F3"], ref["ST"]
    WQ, WK, WV, WO, WU, WD = ref["WQ"], ref["WK"], ref["WV"], ref["WO"], ref["WU"], ref["WD"]
    SD, SC, NP, NPS, NPR = ref["SD"], ref["SC"], ref["NP"], ref["NPS"], ref["NPR"]
    PS, PR, S, R1, R2, R3 = ref["PS"], ref["PR"], ref["S"], ref["R1"], ref["R2"], ref["R3"]
    NG, NV, NR, NZS = ref["NG"], ref["NV"], ref["NR"], ref["NZS"]
    local_sem, entry_s, entry_r = ref["local_sem"], ref["entry_s"], ref["entry_r"]
    pair_s, pair_r, ring_s, ring_r = ref["pair_s"], ref["pair_r"], ref["ring_s"], ref["ring_r"]
    end_s, end_r, norm_s, norm_r = ref["end_s"], ref["end_r"], ref["norm_s"], ref["norm_r"]

    def remote(src, dst, send, recv, device):
        return pltpu.make_async_remote_copy(
            src_ref=src, dst_ref=dst, send_sem=send, recv_sem=recv, device_id=device, device_id_type=MESH
        )

    my_rows, other_rows = pl.ds(c * T, T), pl.ds(o * T, T)
    up_rows = pl.ds(pl.multiple_of(c * D, TILE), D)
    down_rows = pl.ds(pl.multiple_of(c * FH, TILE), FH)
    wo_rows = pl.ds(pl.multiple_of(c * half, TILE), half)
    h2 = T // 2
    plan = [
        ("pair_bias", ref["pair_bias"].at[0:h2, 0:D], F3.at[0:h2, :], None),
        ("pair_bias2", ref["pair_bias"].at[h2:T, T - D : T], F3.at[h2:T, :], None),
        ("tokens", ref["tokens"].at[my_rows, :], XB.at[:, own_half], ref["tokens"].at[other_rows, :]),
        ("wq", ref["wq"], WQ.at[:, own_half], ref["wq"]),
        ("wk", ref["wk"], WK.at[:, own_half], ref["wk"]),
        ("wv", ref["wv"], WV.at[:, own_half], ref["wv"]),
        ("wo", ref["wo"], WO.at[wo_rows, :], ref["wo"]),
        ("og", ref["out_grad"].at[my_rows, :], OG.at[:, own_half], ref["out_grad"].at[other_rows, :]),
        ("wu", ref["wu"], WU.at[up_rows, :], ref["wu"]),
        ("wd", ref["wd"], WD.at[down_rows, :], ref["wd"]),
    ]
    if fused:
        pair_rows = pl.ds(pl.multiple_of(r * sp, 8), sp)
        pair_cols = pl.ds(pl.multiple_of(c * (T // 2), TILE), T // 2)
        plan.append(("pbo", ref["pair_bias"].at[pair_rows, pair_cols], ref["PBO"], None))
    local, cross = {}, {}
    for i, (name, src, dst, away) in enumerate(plan):
        local[name] = pltpu.make_async_copy(src, dst, local_sem.at[i])
        local[name].start()
        if away is not None:
            cross[name] = remote(away, dst, entry_s.at[i], entry_r.at[i], dev_c)
    cross["norms"] = remote(NPS, NPR, entry_s.at[len(plan)], entry_r.at[len(plan)], dev_c)

    NPS[...] = jnp.zeros(NPS.shape, f32)
    for i, name in enumerate(("gi", "si", "gm", "sm")):
        NPS[i : i + 1, :] = ref[name][...]
    barrier = pltpu.get_barrier_semaphore()
    greeted = [dev_c] + ([dev_x, dev_y] + dev_z if fused else [])
    for device in greeted:
        pl.semaphore_signal(barrier, inc=1, device_id=device, device_id_type=MESH)
    pl.semaphore_wait(barrier, len(greeted))
    for name in ("norms", "tokens", "wq", "wk", "wv"):
        cross[name].start()

    def ready(*chosen):
        for name in chosen:
            if name in local:
                local[name].wait()
            if name in cross:
                cross[name].wait()

    seg = ref["segments"][pl.ds(c, 1), :].astype(f32)
    SC[...] = jnp.broadcast_to(seg, (TILE, T)).T
    ready("pair_bias", "pair_bias2")
    row_id = lax.broadcasted_iota(jnp.int32, (TILE, TILE), 0)
    col_id = lax.broadcasted_iota(jnp.int32, (TILE, TILE), 1)
    for a in range(T // TILE):
        rows = slice(a * TILE, (a + 1) * TILE)
        shift = 0 if a * TILE < h2 else T - D
        for b in range(T // TILE):
            cols = slice(b * TILE, (b + 1) * TILE)
            far = abs(a - b) * TILE
            if far - TILE + 1 >= T // 2:
                MM[rows, cols] = jnp.zeros((TILE, TILE), bf16)
                continue
            same = SC[rows, :] == seg[:, cols]
            if far - TILE + 1 >= WIN:
                weight = jnp.ones((TILE, TILE), f32)
            else:
                weight = jnp.exp(F3[rows, b * TILE - shift : (b + 1) * TILE - shift])
                if far + TILE - 1 >= WIN:
                    inside = jnp.abs(row_id - col_id + (a - b) * TILE) < WIN
                    weight = jnp.where(inside, weight, 1.0)
            MM[rows, cols] = jnp.where(same, weight, 0.0).astype(bf16)

    ready("norms")
    for i in range(4):
        NP[i : i + 1, own_half] = NPS[i : i + 1, :]
        NP[i : i + 1, other_half] = NPR[i : i + 1, :]
    step_rows = 256
    ready("tokens")

    def norm_in(i, carry):
        rows = pl.ds(i * step_rows, step_rows)
        x = XB[rows, :].astype(f32)
        centred = x - jnp.mean(x, axis=1, keepdims=True)
        inv = lax.rsqrt(jnp.mean(centred * centred, axis=1, keepdims=True) + EPSILON)
        t = centred * inv
        F1[rows, :] = x
        XB[rows, :] = t.astype(bf16)
        HN[rows, :] = (t * NP[0:1, :] + NP[1:2, :]).astype(bf16)
        ST[rows, 0:1] = inv
        return carry

    lax.fori_loop(0, T // step_rows, norm_in, 0)
    for name in ("wo", "og", "wu", "wd"):
        cross[name].start()
    ready("wq", "wk", "wv")

    for j in range(D // COLS):
        cols = slice(j * COLS, (j + 1) * COLS)
        late = slice(D + j * COLS, D + (j + 1) * COLS)
        e = jnp.exp(dot(HN[...], WK[:, cols]))
        a = (e * dot(HN[...], WV[:, cols])).astype(bf16)
        AB[:, cols] = a
        AB[:, late] = e.astype(bf16)
        gate = jax.nn.sigmoid(dot(HN[...], WQ[:, cols]))
        inv = 1.0 / dot(MM[...], AB[:, late])
        ratio = dot(MM[...], AB[:, cols]) * inv
        y = gate * ratio
        Y[:, cols] = y.astype(bf16)
        QQ[:, cols] = (y * (1.0 - gate)).astype(bf16)
        RT[:, cols] = ratio.astype(bf16)
        RZ[:, cols] = (gate * inv).astype(bf16)

    ready("wo")
    F1[...] += dot(Y[...], WO[...])

    def norm_mid(i, carry):
        rows = pl.ds(i * step_rows, step_rows)
        x = F1[rows, :]
        centred = x - jnp.mean(x, axis=1, keepdims=True)
        inv = lax.rsqrt(jnp.mean(centred * centred, axis=1, keepdims=True) + EPSILON)
        t = centred * inv
        T2[rows, :] = t.astype(bf16)
        G[rows, :] = (t * NP[2:3, :] + NP[3:4, :]).astype(bf16)
        ST[rows, 1:2] = inv
        F3[rows, :] = jnp.zeros((step_rows, D), f32)
        return carry

    lax.fori_loop(0, T // step_rows, norm_mid, 0)
    ready("og", "wu", "wd", "pbo")

    order = {
        0: lambda b: b if not fused else ((b % 2) * 2 + (b // 2) % 2) * nz + b // 4,
        1: lambda b: b if not fused else (((b // 2) % 2) * 2 + b % 2) * nz + b // 4,
    }
    route = {0: (mx, dev_x, my, dev_y), 1: (my, dev_y, mx, dev_x)}

    def form(k, part, height, own, at=0):
        slot, pslot = k % SLOTS, k % 2
        width = own.shape[1]
        for b in range(nb):
            rows = slice(b * height, (b + 1) * height)
            total = own[rows, :].astype(f32) + PR[pslot, part, rows, at : at + width].astype(f32)
            S[slot, part, order[part](b), 0:height, at : at + width] = total.astype(bf16)

    def first(k, part, height):
        slot = k % SLOTS
        b1, d1, _, _ = route[part]
        return remote(
            S.at[slot, part, pl.ds((1 - b1) * 2 * nz, 2 * nz), pl.ds(0, height), :],
            R1.at[slot, part, :, pl.ds(0, height), :],
            ring_s.at[slot, part], ring_r.at[slot, part], d1,
        )

    def second(k, part, height):
        slot = k % SLOTS
        b1, _, b2, d2 = route[part]
        return remote(
            S.at[slot, part, pl.ds(b1 * 2 * nz + (1 - b2) * nz, nz), pl.ds(0, height), :],
            R2.at[slot, part, :, pl.ds(0, height), :],
            ring_s.at[slot, 2 + part], ring_r.at[slot, 2 + part], d2,
        )

    def third(k, part, height):
        slot = k % SLOTS
        b1, _, b2, _ = route[part]
        copies = []
        for j in range(1, nz):
            sem = 4 + part * (nz - 1) + j - 1
            copies.append(remote(
                S.at[slot, part, b1 * 2 * nz + b2 * nz + lax.rem(mz + j, nz), pl.ds(0, height), :],
                R3.at[slot, part, j - 1, pl.ds(0, height), :],
                ring_s.at[slot, sem], ring_r.at[slot, sem], dev_z[j - 1],
            ))
        return copies

    def whole(k):
        return pltpu.make_async_copy(S.at[k % SLOTS], ref["GO"].at[k], ring_s.at[k % SLOTS, 0])

    def start_sum(k, height):
        if not fused:
            whole(k).start()
            return
        for part in range(2):
            first(k, part, height).start()

    def after_first(k, height):
        if not fused:
            whole(k).wait()
            return
        slot = k % SLOTS
        for part in range(2):
            b1, _, _, _ = route[part]
            first(k, part, height).wait()
            keep = pl.ds(b1 * 2 * nz, 2 * nz)
            total = S[slot, part, keep, 0:height, :].astype(f32) + R1[slot, part, :, 0:height, :].astype(f32)
            S[slot, part, keep, 0:height, :] = total.astype(bf16)
            second(k, part, height).start()

    def after_second(k, height):
        if not fused:
            return
        slot = k % SLOTS
        for part in range(2):
            b1, _, b2, _ = route[part]
            second(k, part, height).wait()
            keep = pl.ds(b1 * 2 * nz + b2 * nz, nz)
            total = S[slot, part, keep, 0:height, :].astype(f32) + R2[slot, part, :, 0:height, :].astype(f32)
            S[slot, part, keep, 0:height, :] = total.astype(bf16)
            for copy in third(k, part, height):
                copy.start()

    def after_third(k, height, put):
        if not fused:
            return
        slot = k % SLOTS
        for part in range(2):
            b1, _, b2, _ = route[part]
            for copy in third(k, part, height):
                copy.wait()
            total = S[slot, part, b1 * 2 * nz + b2 * nz + mz, 0:height, :].astype(f32)
            for j in range(nz - 1):
                total = total + R3[slot, part, j, 0:height, :].astype(f32)
            put(k, part, total)

    def upright(v):
        filled = jnp.concatenate([v, jnp.zeros((TILE - v.shape[0], v.shape[1]), f32)], 0)
        return filled.T[:, : v.shape[0]]

    def put_hidden(k, part, total):
        at = pl.ds(pl.multiple_of(k * COLS, COLS), COLS)
        if part == 0:
            ref["o_up"][:, at] = total
        else:
            ref["o_dn"][at, :] = upright(total)

    def hidden_step(owner, i):
        cols = pl.ds(pl.multiple_of(i * COLS, COLS), COLS)
        up_at = pl.ds(pl.multiple_of(owner * D, TILE), D)
        down_at = pl.ds(pl.multiple_of(owner * FH + i * COLS, COLS), COLS)
        s, slope = gelu_pair(dot(G[...], WU[up_at, cols]))
        SD[:, 0:COLS] = s.astype(bf16)
        SD[:, COLS:] = (dot_nt(OG[...], WD[down_at, :]) * slope).astype(bf16)
        F1[...] += dot(SD[:, 0:COLS], WD[down_at, :])
        F3[...] += dot_nt(SD[:, COLS:], WU[up_at, cols])
        return dot_tn(G[...], SD[:, COLS:]), dot_tn(OG[...], SD[:, 0:COLS])

    def pair_copy(k, height):
        slot = k % 2
        return remote(
            PS.at[slot, :, pl.ds(0, height), :], PR.at[slot, :, pl.ds(0, height), :],
            pair_s.at[slot, 0], pair_r.at[slot, 0], dev_c,
        )

    def hidden_block(i, carry):
        slot = lax.rem(i, 2)
        up, down = hidden_step(o, i)
        PS[slot, 0, 0:D, :] = up.astype(bf16)
        PS[slot, 1, 0:D, :] = down.astype(bf16)
        pair_copy(i, D).start()
        up, down = hidden_step(c, i)
        pair_copy(i, D).wait()
        form(i, 0, sh, up)
        form(i, 1, sh, down)
        start_sum(i, sh)
        pl.when(i >= 1)(lambda: after_first(i - 1, sh))
        pl.when(i >= 2)(lambda: after_second(i - 2, sh))
        pl.when(i >= 3)(lambda: after_third(i - 3, sh, put_hidden))
        return carry

    lax.fori_loop(0, blocks, hidden_block, 0)

    def finish_out(i, carry):
        rows = pl.ds(i * step_rows, step_rows)
        G[rows, :] = F1[rows, :].astype(bf16)
        return carry

    lax.fori_loop(0, T // step_rows, finish_out, 0)
    blk_local = pltpu.make_async_copy(G.at[:, own_half], ref["o_blk"].at[my_rows, :], local_sem.at[12])
    blk_cross = remote(G.at[:, other_half], ref["o_blk"].at[my_rows, :], end_s.at[0], end_r.at[0], dev_c)
    blk_local.start()
    blk_cross.start()

    NG[...] = jnp.zeros(NG.shape, f32)

    def norm_mid_back(i, carry):
        rows = pl.ds(i * step_rows, step_rows)
        grad, t = F3[rows, :], T2[rows, :].astype(f32)
        w = grad * NP[2:3, :]
        mean_w = jnp.mean(w, axis=1, keepdims=True)
        mean_wt = jnp.mean(w * t, axis=1, keepdims=True)
        dx = OG[rows, :].astype(f32) + ST[rows, 1:2] * (w - mean_w - t * mean_wt)
        F3[rows, :] = dx
        T2[rows, :] = dx.astype(bf16)
        NG[2] += fold_rows(grad * t)
        NG[3] += fold_rows(grad)
        return carry

    lax.fori_loop(0, T // step_rows, norm_mid_back, 0)
    last = blocks - 1
    after_first(last, sh)
    after_second(last - 1, sh)
    after_third(last - 2, sh, put_hidden)

    NZ = WU
    for j in range(D // COLS):
        cols = slice(j * COLS, (j + 1) * COLS)
        late = slice(D + j * COLS, D + (j + 1) * COLS)
        dm = dot_nt(T2[...], WO[cols, :])
        WD[0:T, cols] = (dm * QQ[:, cols].astype(f32)).astype(bf16)
        dn = dm * RZ[:, cols].astype(f32)
        NZ[0:T, cols] = dn.astype(bf16)
        NZ[0:T, late] = (-dn * RT[:, cols].astype(f32)).astype(bf16)
    OG[0:D, :] = dot_tn(T2[...], Y[...]).astype(bf16)
    QQ[0:D, :] = dot_tn(HN[...], WD[0:T, :]).astype(bf16)

    sources = (OG, QQ, RZ, RT)

    def pieces(part_no):
        found, at = [], part_no * COLS
        while at < (part_no + 1) * COLS:
            source, off = at // half, at % half
            width = min(half - off, (part_no + 1) * COLS - at)
            found.append((source, off, width, at - part_no * COLS))
            at += width
        return found

    def late_copies(k, first_part):
        slot, copies = k % 2, []
        for part in range(2):
            for source, off, width, at in pieces(first_part + part):
                cols = pl.ds(pl.multiple_of(o * half + off, TILE), width)
                copies.append(remote(
                    sources[source].at[pl.ds(0, D), cols], PR.at[slot, part, pl.ds(0, D), pl.ds(at, width)],
                    pair_s.at[slot, 1 + len(copies)], pair_r.at[slot, 1 + len(copies)], dev_c,
                ))
        return copies

    def late_form(k, first_part, copies):
        for copy in copies:
            copy.wait()
        for part in range(2):
            for source, off, width, at in pieces(first_part + part):
                cols = pl.ds(pl.multiple_of(c * half + off, TILE), width)
                form(k, part, sh, sources[source][0:D, cols], at)

    def put_late(first_part):
        def put(k, part, total):
            for source, off, width, at in pieces(first_part + part):
                value = total[:, at : at + width]
                if source == 0:
                    ref["o_wo"][off : off + width, :] = upright(value)
                else:
                    ref[("o_q", "o_k", "o_v")[source - 1]][:, off : off + width] = value
        return put

    k0, k1, k2, k3 = blocks, blocks + 1, blocks + 2, blocks + 3
    sent = late_copies(k0, 0)
    for copy in sent:
        copy.start()

    for j in range(T // COLS):
        cols = slice(j * COLS, (j + 1) * COLS)
        low, high = max(0, (j - 1) * COLS), min(T, (j + 2) * COLS)
        target = PS.at[j // 2, j % 2]
        for start, stop in ((0, low), (high, T)):
            if stop > start:
                target[start:stop, :] = jnp.zeros((stop - start, COLS), bf16)
        grad = dot_nt(NZ[low:high, :], AB[cols, :])
        for t in range(COLS // TILE):
            at = j * COLS + t * TILE
            same = SC[low:high, :] == seg[:, at : at + TILE]
            gap = (
                lax.broadcasted_iota(jnp.int32, (high - low, TILE), 0)
                - lax.broadcasted_iota(jnp.int32, (high - low, TILE), 1)
                + (low - at)
            )
            kept = jnp.where(same & (jnp.abs(gap) < WIN), grad[:, t * TILE : (t + 1) * TILE], 0.0)
            target[low:high, t * TILE : (t + 1) * TILE] = kept.astype(bf16)

    late_form(k0, 0, sent)
    start_sum(k0, sh)
    after_second(last, sh)
    after_third(last - 1, sh, put_hidden)

    def mixer_copy():
        return remote(PS.at[o], PR.at[k1 % 2], pair_s.at[k1 % 2, 0], pair_r.at[k1 % 2, 0], dev_c)

    mixer_copy().start()

    for j in range(D // COLS):
        cols = slice(j * COLS, (j + 1) * COLS)
        late = slice(D + j * COLS, D + (j + 1) * COLS)
        da = dot_tn(MM[...], NZ[0:T, cols])
        db = dot_tn(MM[...], NZ[0:T, late])
        e = AB[:, late].astype(f32)
        WD[T : 2 * T, cols] = (db * e + da * AB[:, cols].astype(f32)).astype(bf16)
        WD[2 * T : 3 * T, cols] = (da * e).astype(bf16)
    RZ[0:D, :] = dot_tn(HN[...], WD[T : 2 * T, :]).astype(bf16)

    mixer_copy().wait()
    for part in range(2):
        form(k1, part, sp, PS.at[c, part][...])
    start_sum(k1, sp)
    after_first(k0, sh)
    after_third(last, sh, put_hidden)

    sent = late_copies(k2, 2)
    for copy in sent:
        copy.start()
    RT[0:D, :] = dot_tn(HN[...], WD[2 * T : 3 * T, :]).astype(bf16)
    late_form(k2, 2, sent)
    start_sum(k2, sh)
    after_first(k1, sp)
    after_second(k0, sh)
    sent = late_copies(k3, 4)
    for copy in sent:
        copy.start()

    for j in range(D // COLS):
        cols = slice(j * COLS, (j + 1) * COLS)
        F1[:, cols] = (
            dot_nt(WD[0:T, :], WQ[cols, :])
            + dot_nt(WD[T : 2 * T, :], WK[cols, :])
            + dot_nt(WD[2 * T : 3 * T, :], WV[cols, :])
        )
    late_form(k3, 4, sent)
    start_sum(k3, sh)

    def norm_in_back(i, carry):
        rows = pl.ds(i * step_rows, step_rows)
        grad, t = F1[rows, :], XB[rows, :].astype(f32)
        w = grad * NP[0:1, :]
        mean_w = jnp.mean(w, axis=1, keepdims=True)
        mean_wt = jnp.mean(w * t, axis=1, keepdims=True)
        F3[rows, :] = F3[rows, :] + ST[rows, 0:1] * (w - mean_w - t * mean_wt)
        NG[0] += fold_rows(grad * t)
        NG[1] += fold_rows(grad)
        return carry

    lax.fori_loop(0, T // step_rows, norm_in_back, 0)
    tok_local = pltpu.make_async_copy(F3.at[:, own_half], ref["o_tok"].at[my_rows, :], local_sem.at[13])
    tok_cross = remote(F3.at[:, other_half], ref["o_tok"].at[my_rows, :], end_s.at[1], end_r.at[1], dev_c)
    tok_local.start()
    tok_cross.start()

    NV[...] = jnp.zeros(NV.shape, f32)
    for i in range(4):
        NV[i : i + 1, :] = jnp.sum(NG[i], axis=0, keepdims=True)
    copy = remote(NV.at[:, other_half], NR.at[0], norm_s.at[0], norm_r.at[0], dev_c)
    copy.start()
    copy.wait()
    NR[1] = NV[:, own_half] + NR[0]
    if fused:
        def put_pair(k, part, total):
            cols = slice(part * COLS, (part + 1) * COLS)
            ref["o_pair"][:, cols] = total * jnp.exp(ref["PBO"][:, cols])

        copy = remote(NR.at[1], NR.at[2], norm_s.at[1], norm_r.at[1], dev_x)
        copy.start()
        after_first(k2, sh)
        after_second(k1, sp)
        after_third(k0, sh, put_late(0))
        copy.wait()
        NR[3] = NR[1] + NR[2]
        copy = remote(NR.at[3], NR.at[4], norm_s.at[2], norm_r.at[2], dev_y)
        copy.start()
        after_first(k3, sh)
        after_second(k2, sh)
        after_third(k1, sp, put_pair)
        copy.wait()
        total = NR[3] + NR[4]
        NZS[mz] = total
        copies = [
            remote(NZS.at[mz], NZS.at[mz], norm_s.at[2 + j], norm_r.at[2 + j], dev_z[j - 1])
            for j in range(1, nz)
        ]
        for copy in copies:
            copy.start()
        after_second(k3, sh)
        after_third(k2, sh, put_late(2))
        for copy in copies:
            copy.wait()
        total = NZS[0]
        for j in range(1, nz):
            total = total + NZS[j]
        for i, name in enumerate(("o_gi", "o_si", "o_gm", "o_sm")):
            ref[name][...] = total[i : i + 1, :]
        after_third(k3, sh, put_late(4))
    else:
        ref["o_norm"][...] = NR[1]
        for k in (k2, k3):
            after_first(k, sh)
    blk_local.wait()
    blk_cross.wait()
    tok_local.wait()
    tok_cross.wait()


def run_block(T, D, FH, R, args):
    half = D // 2
    blocks = FH // COLS
    fused = R % 4 == 0 and (D // R) % 16 == 0 and D % R == 0 and (T // R) % 16 == 0 and T % R == 0
    nb = R if fused else 16
    nz = nb // 4
    sh, sp = D // nb, T // nb
    any_spec, vmem = pl.BlockSpec(memory_space=pl.ANY), pl.BlockSpec(memory_space=pltpu.VMEM)
    inputs = {
        "tokens": any_spec, "segments": vmem, "gi": vmem, "si": vmem, "wq": any_spec, "wk": any_spec,
        "wv": any_spec, "wo": any_spec, "gm": vmem, "sm": vmem, "wu": any_spec, "wd": any_spec,
        "pair_bias": any_spec, "out_grad": any_spec,
    }
    outputs = {"o_blk": (any_spec, (2 * T, half), bf16), "o_tok": (any_spec, (2 * T, half), f32)}
    if fused:
        for name in ("o_gi", "o_si", "o_gm", "o_sm"):
            outputs[name] = (vmem, (1, half), f32)
        for name in ("o_q", "o_k", "o_v"):
            outputs[name] = (vmem, (sh, half), f32)
        outputs["o_wo"] = (vmem, (half, sh), f32)
        outputs["o_up"] = (vmem, (sh, FH), f32)
        outputs["o_dn"] = (vmem, (FH, sh), f32)
        outputs["o_pair"] = (vmem, (sp, T // 2), f32)
    else:
        outputs["o_norm"] = (vmem, (8, half), f32)
        outputs["GO"] = (any_spec, (blocks + 4, 2, nb, sp, COLS), bf16)
    wide = (T, D)
    scratch = {name: pltpu.VMEM(wide, bf16) for name in ("XB", "OG", "HN", "G", "Y", "QQ", "RT", "RZ", "T2")}
    scratch |= {
        "AB": pltpu.VMEM((T, 2 * D), bf16), "MM": pltpu.VMEM((T, T), bf16),
        "F1": pltpu.VMEM(wide, f32), "F3": pltpu.VMEM(wide, f32), "ST": pltpu.VMEM((T, TILE), f32),
        "WQ": pltpu.VMEM((D, D), bf16), "WK": pltpu.VMEM((D, D), bf16), "WV": pltpu.VMEM((D, D), bf16),
        "WO": pltpu.VMEM((D, D), bf16), "WU": pltpu.VMEM((2 * D, FH), bf16), "WD": pltpu.VMEM((2 * FH, D), bf16),
        "SD": pltpu.VMEM((T, 2 * COLS), bf16), "SC": pltpu.VMEM((T, TILE), f32),
        "NP": pltpu.VMEM((8, D), f32), "NPS": pltpu.VMEM((8, half), f32), "NPR": pltpu.VMEM((8, half), f32),
        "PS": pltpu.VMEM((2, 2, T, COLS), bf16), "PR": pltpu.VMEM((2, 2, T, COLS), bf16),
        "S": pltpu.VMEM((SLOTS, 2, nb, sp, COLS), bf16),
        "R1": pltpu.VMEM((SLOTS, 2, 2 * nz, sp, COLS), bf16) if fused else pltpu.VMEM((8, TILE), f32),
        "R2": pltpu.VMEM((SLOTS, 2, nz, sp, COLS), bf16) if fused else pltpu.VMEM((8, TILE), f32),
        "R3": pltpu.VMEM((SLOTS, 2, nz - 1, sp, COLS), bf16) if fused else pltpu.VMEM((8, TILE), f32),
        "NG": pltpu.VMEM((4, 8, D), f32), "NV": pltpu.VMEM((8, D), f32), "NR": pltpu.VMEM((5, 8, half), f32),
        "NZS": pltpu.VMEM((nz, 8, half), f32), "PBO": pltpu.VMEM((sp, T // 2), f32),
        "local_sem": pltpu.SemaphoreType.DMA((16,)),
        "entry_s": pltpu.SemaphoreType.DMA((16,)), "entry_r": pltpu.SemaphoreType.DMA((16,)),
        "pair_s": pltpu.SemaphoreType.DMA((2, 5)), "pair_r": pltpu.SemaphoreType.DMA((2, 5)),
        "ring_s": pltpu.SemaphoreType.DMA((SLOTS, 4 + 2 * nz)), "ring_r": pltpu.SemaphoreType.DMA((SLOTS, 4 + 2 * nz)),
        "end_s": pltpu.SemaphoreType.DMA((2,)), "end_r": pltpu.SemaphoreType.DMA((2,)),
        "norm_s": pltpu.SemaphoreType.DMA((2 + nz,)), "norm_r": pltpu.SemaphoreType.DMA((2 + nz,)),
    }
    names = tuple(inputs) + tuple(outputs) + tuple(scratch)
    results = pl.pallas_call(
        functools.partial(block_kernel, T, D, FH, R, fused, names),
        out_shape=tuple(jax.ShapeDtypeStruct(shape, kind) for _, shape, kind in outputs.values()),
        in_specs=list(inputs.values()),
        out_specs=tuple(spec for spec, _, _ in outputs.values()),
        scratch_shapes=list(scratch.values()),
        compiler_params=pltpu.CompilerParams(
            collective_id=0, has_side_effects=True, vmem_limit_bytes=63 << 20
        ),
    )(*args)
    out = dict(zip(outputs, results))
    if fused:
        return out
    parts = out.pop("GO")
    height = lambda v, rows: v.reshape(nb, sp, v.shape[-1])[:, : rows // nb].reshape(rows, v.shape[-1])
    join = lambda chosen: jnp.concatenate(chosen, 1).astype(f32)
    scatter = lambda v: lax.psum_scatter(v, "rows", scatter_dimension=0, tiled=True)
    out["o_up"] = scatter(join([height(parts[k, 0], D) for k in range(blocks)]))
    out["o_dn"] = scatter(join([height(parts[k, 1], D) for k in range(blocks)])).T
    late = join([height(parts[k, p], D) for k in (blocks, blocks + 2, blocks + 3) for p in range(2)])
    cut = [scatter(late[:, i * half : (i + 1) * half]) for i in range(4)]
    out["o_wo"], out["o_q"], out["o_k"], out["o_v"] = cut[0].T, cut[1], cut[2], cut[3]
    pair = scatter(join([height(parts[blocks + 1, p], T) for p in range(2)]))
    bias = lax.dynamic_slice(
        args[12], (lax.axis_index("rows") * pair.shape[0], lax.axis_index("chan") * (T // 2)), pair.shape
    )
    out["o_pair"] = pair * jnp.exp(bias)
    norms = lax.psum(out["o_norm"], "rows")
    for i, name in enumerate(("o_gi", "o_si", "o_gm", "o_sm")):
        out[name] = norms[i : i + 1]
    return out


def on_device(
    tokens, segments, gain_in, shift_in, query_weight, key_weight, value_weight, out_weight,
    gain_mid, shift_mid, up_weight, down_weight, pair_bias, out_grad,
):
    T = segments.shape[1]
    D, FH = up_weight.shape
    R = lax.axis_size("rows")
    row = lambda v: v.reshape(1, v.shape[0])
    out = run_block(T, D, FH, R, (
        tokens, segments, row(gain_in), row(shift_in), query_weight, key_weight, value_weight, out_weight,
        row(gain_mid), row(shift_mid), up_weight, down_weight, pair_bias, out_grad,
    ))
    flat = lambda name: out[name].reshape(out[name].shape[1])
    return (
        out["o_blk"], out["o_tok"], flat("o_gi"), flat("o_si"), out["o_q"], out["o_k"], out["o_v"], out["o_wo"],
        flat("o_gm"), flat("o_sm"), out["o_up"], out["o_dn"], out["o_pair"],
    )


def solution(mesh):
    split, first, second = P("rows", "chan"), P("chan", None), P(None, "chan")
    return jax.shard_map(
        on_device,
        mesh=mesh,
        in_specs=(
            split, P("rows", None), P("chan"), P("chan"), second, second, second, first,
            P("chan"), P("chan"), second, first, P(), split,
        ),
        out_specs=(
            split, split, P("chan"), P("chan"), split, split, split, P("chan", "rows"),
            P("chan"), P("chan"), split, P("chan", "rows"), split,
        ),
        check_vma=False,
    )
```

time: 1220 us -> 145 us (0.12); the launches traced: 1200 us -> 145 us
  waiting for transfers between devices: 839 us -> 0 us
  matrix products: 161 us -> 0 us
  Pallas kernels: 0 us -> 123 us
  blocking collectives: 59.7 us -> 0 us
  local copies, waits for them, and re-layouts: 65.7 us -> 16.4 us
  other arithmetic: 54.4 us -> 5.1 us
  between operations: 14.5 us -> 0.69 us
    reduce_scatter x8 -> x0, waiting for transfers between devices: 787 us -> none  [the longest x1 142 us: on_device(): lax.psum_scatter(up_grad, 'rows', scatter_dimension=0, tiled=True)]
    dot_general x21 -> x0, matrix products: 161 us -> none  [the longest x1 33.7 us: on_device(): pre_act = jnp.dot(full_mid, up_weight, preferred_element_type=jnp.float32)]
    pallas_call x0 -> x1, Pallas kernels: none -> 123 us  [run_block(): pl.pallas_call(functools.partial(block_kernel, T, D, FH, R, fused, names)...]
    psum x7 -> x0, blocking collectives: 59.7 us -> none  [the longest x1 42.9 us: on_device(): lax.psum(jnp.stack([gain_in_part, shift_in_part, gain_mid_part, shift_mid...]
    unnamed x72 -> x21, local copies, waits for them, and re-layouts: 49.4 us -> 11.4 us
    all_gather x4 -> x0, waiting for transfers between devices: 36.7 us -> none  [the longest x2 23.3 us: normalize(): gathered = lax.all_gather(norm_out, 'chan', axis=1, tiled=True)]
    convert_element_type x7 -> x0, other arithmetic: 26.2 us -> none  [the longest x1 6.29 us: on_device(): value_low = (kv_grad * raised_keys).astype(jnp.bfloat16)]
    reduce_sum x6 -> x0, other arithmetic: 15.5 us -> none  [the longest x2 6.3 us: normalize_back(): return (back_rows, jnp.sum(grad_rows * normed, 0), jnp.sum(grad_rows, 0))]
  transfers between devices with their start and end apart: 16 -> 0, of which waited for: 12 -> 0; matrix products, arithmetic and copies ran while one was open for 12% -> 0% of each run, Pallas kernels for 0% -> 0%
where the time goes in v1:
time: 145 us
  Pallas kernels  123 us (85%)
  local copies, waits for them, and re-layouts  16.4 us (11%)
  other arithmetic  5.1 us (4%)
    pallas_call x1, Pallas kernels, run_block(): pl.pallas_call(functools.partial(block_kernel, T, D, FH, R, fused, names)...  123 us
    unnamed x21, local copies, waits for them, and re-layouts  11.4 us
    pallas_call x4, other arithmetic, run_block(): pl.pallas_call(functools.partial(block_kernel, T, D, FH, R, fused, names)...  5.1 us
    reshape x4, local copies, waits for them, and re-layouts, on_device(): row = lambda v: v.reshape(1, v.shape[0])  4.98 us

profile of v1, /device:TPU:0, one launch (start us, length us, event | category | flops | bytes accessed | tf_op | source)
XLA Modules:
  0.0 144.8 jit_solution(1587286424118214968)
XLA Ops:
  0.6 1.2 reshape.50.all_refs_2_
  1.9 1.2 reshape.51.all_refs_3_
  3.1 1.2 reshape.52.all_refs_8_
  4.4 1.2 reshape.53.all_refs_9_
  5.6 122.6 %shard_map.237 = (bf16[2048,384]{1,0:T(8,128)(2,1)}, f32[2048,384]{1,0:T(8,128)}, f32[1,384]{1,0:T(1,128)}, f32[1,384]{1,0:T(1,128)}, f32[1,384]{1,0:T(1,128)}, ...) custom-call(bf16[2048,384]{1,0:T(8,128)(2,1)} %all_refs_0_.1, ...), custom_call_target="tpu_custom_call" | custom-call | tf_op jit(solution)/shard_map/pallas_call | solution.py:622
  128.3 0.0 copy-start
  128.3 1.4 reduce
  129.7 1.3 reduce.1
  131.0 1.2 reduce.2
  132.2 1.2 reduce.3
  133.4 1.7 %copy.27 = f32[384,48]{0,1:T(8,128)} copy(f32[384,48]{1,0:T(8,128)} %get-tuple-element.46) | data formatting | bytes 147456
  135.1 2.1 %copy.28 = f32[1536,48]{0,1:T(8,128)} copy(f32[1536,48]{1,0:T(8,128)} %get-tuple-element.50) | data formatting | bytes 589824
  137.2 2.7 %copy.36 = bf16[2048,384]{1,0:T(8,128)(2,1)} copy(bf16[2048,384]{1,0:T(8,128)(2,1)} %get-tuple-element.65) | data formatting | bytes 3145728
  139.9 0.0 copy-done
  139.9 0.0 copy-start.5
  139.9 0.0 copy-start.4
  139.9 0.0 copy-start.3
  139.9 0.0 copy-start.1
  139.9 0.0 copy-start.2
  139.9 1.7 %copy.37 = f32[2048,384]{1,0:T(8,128)} copy(f32[2048,384]{1,0:T(8,128)S(1)} %copy-done) | data formatting | bytes 6291456
  141.6 0.0 copy-done.5
  141.6 0.6 copy.38
  142.2 0.0 copy-done.4
  142.2 0.6 copy.39
  142.8 0.0 copy-done.3
  142.8 0.6 copy.40
  143.5 0.0 copy-done.1
  143.5 0.7 copy.41
  144.2 0.0 copy-done.2
  144.2 0.7 copy.42
Async XLA Ops:
  128.3 11.6 %copy-start = (f32[2048,384]{1,0:T(8,128)S(1)}, f32[2048,384]{1,0:T(8,128)}, u32[]{:S(2)}) copy-start(f32[2048,384]{1,0:T(8,128)} %get-tuple-element.66) | copy-start | bytes 9437188
  139.9 1.7 %copy-start.5 = (f32[48,384]{1,0:T(8,128)S(1)}, f32[48,384]{1,0:T(8,128)}, u32[]{:S(2)}) copy-start(f32[48,384]{1,0:T(8,128)} %get-tuple-element.69) | copy-start | bytes 221188
  139.9 2.3 %copy-start.4 = (f32[48,384]{1,0:T(8,128)S(1)}, f32[48,384]{1,0:T(8,128)}, u32[]{:S(2)}) copy-start(f32[48,384]{1,0:T(8,128)} %get-tuple-element.70) | copy-start | bytes 221188
  139.9 3.0 %copy-start.3 = (f32[48,384]{1,0:T(8,128)S(1)}, f32[48,384]{1,0:T(8,128)}, u32[]{:S(2)}) copy-start(f32[48,384]{1,0:T(8,128)} %get-tuple-element.71) | copy-start | bytes 221188
  139.9 3.6 %copy-start.1 = (f32[48,1536]{1,0:T(8,128)S(1)}, f32[48,1536]{1,0:T(8,128)}, u32[]{:S(2)}) copy-start(f32[48,1536]{1,0:T(8,128)} %get-tuple-element.75) | copy-start | bytes 884740
  139.9 4.3 %copy-start.2 = (f32[64,512]{1,0:T(8,128)S(1)}, f32[64,512]{1,0:T(8,128)}, u32[]{:S(2)}) copy-start(f32[64,512]{1,0:T(8,128)} %get-tuple-element.77) | copy-start | bytes 393220

commit v2 on v1

--- a/solution.py
+++ b/solution.py
@@ -63,6 +63,7 @@
     SD, SC, NP, NPS, NPR = ref["SD"], ref["SC"], ref["NP"], ref["NPS"], ref["NPR"]
     PS, PR, S, R1, R2, R3 = ref["PS"], ref["PR"], ref["S"], ref["R1"], ref["R2"], ref["R3"]
     NG, NV, NR, NZS = ref["NG"], ref["NV"], ref["NR"], ref["NZS"]
+    FIN, fin_sem = ref["FIN"], ref["fin_sem"]
     local_sem, entry_s, entry_r = ref["local_sem"], ref["entry_s"], ref["entry_r"]
     pair_s, pair_r, ring_s, ring_r = ref["pair_s"], ref["pair_r"], ref["ring_s"], ref["ring_r"]
     end_s, end_r, norm_s, norm_r = ref["end_s"], ref["end_r"], ref["norm_s"], ref["norm_r"]
@@ -103,7 +104,7 @@
 
     NPS[...] = jnp.zeros(NPS.shape, f32)
     for i, name in enumerate(("gi", "si", "gm", "sm")):
-        NPS[i : i + 1, :] = ref[name][...]
+        NPS[i : i + 1, :] = ref[name][...].reshape(1, half)
     barrier = pltpu.get_barrier_semaphore()
     greeted = [dev_c] + ([dev_x, dev_y] + dev_z if fused else [])
     for device in greeted:
@@ -282,7 +283,7 @@
             for copy in third(k, part, height):
                 copy.start()
 
-    def after_third(k, height, put):
+    def after_third(k, height):
         if not fused:
             return
         slot = k % SLOTS
@@ -293,18 +294,15 @@
             total = S[slot, part, b1 * 2 * nz + b2 * nz + mz, 0:height, :].astype(f32)
             for j in range(nz - 1):
                 total = total + R3[slot, part, j, 0:height, :].astype(f32)
-            put(k, part, total)
-
-    def upright(v):
-        filled = jnp.concatenate([v, jnp.zeros((TILE - v.shape[0], v.shape[1]), f32)], 0)
-        return filled.T[:, : v.shape[0]]
-
-    def put_hidden(k, part, total):
-        at = pl.ds(pl.multiple_of(k * COLS, COLS), COLS)
-        if part == 0:
-            ref["o_up"][:, at] = total
-        else:
-            ref["o_dn"][at, :] = upright(total)
+            if height != sh:
+                total = total * jnp.exp(ref["PBO"][:, part * COLS : (part + 1) * COLS])
+            FIN[k, part, 0:height, :] = total
+            fin_copy(k, part, height).start()
+
+    def fin_copy(k, part, height):
+        return pltpu.make_async_copy(
+            FIN.at[k, part, pl.ds(0, height), :], ref["o_fin"].at[k, part, pl.ds(0, height), :], fin_sem.at[k, part]
+        )
 
     def hidden_step(owner, i):
         cols = pl.ds(pl.multiple_of(i * COLS, COLS), COLS)
@@ -337,7 +335,7 @@
         start_sum(i, sh)
         pl.when(i >= 1)(lambda: after_first(i - 1, sh))
         pl.when(i >= 2)(lambda: after_second(i - 2, sh))
-        pl.when(i >= 3)(lambda: after_third(i - 3, sh, put_hidden))
+        pl.when(i >= 3)(lambda: after_third(i - 3, sh))
         return carry
 
     lax.fori_loop(0, blocks, hidden_block, 0)
@@ -372,7 +370,7 @@
     last = blocks - 1
     after_first(last, sh)
     after_second(last - 1, sh)
-    after_third(last - 2, sh, put_hidden)
+    after_third(last - 2, sh)
 
     NZ = WU
     for j in range(D // COLS):
@@ -388,14 +386,7 @@
 
     sources = (OG, QQ, RZ, RT)
 
-    def pieces(part_no):
-        found, at = [], part_no * COLS
-        while at < (part_no + 1) * COLS:
-            source, off = at // half, at % half
-            width = min(half - off, (part_no + 1) * COLS - at)
-            found.append((source, off, width, at - part_no * COLS))
-            at += width
-        return found
+    pieces = functools.partial(late_pieces, half)
 
     def late_copies(k, first_part):
         slot, copies = k % 2, []
@@ -415,16 +406,6 @@
             for source, off, width, at in pieces(first_part + part):
                 cols = pl.ds(pl.multiple_of(c * half + off, TILE), width)
                 form(k, part, sh, sources[source][0:D, cols], at)
-
-    def put_late(first_part):
-        def put(k, part, total):
-            for source, off, width, at in pieces(first_part + part):
-                value = total[:, at : at + width]
-                if source == 0:
-                    ref["o_wo"][off : off + width, :] = upright(value)
-                else:
-                    ref[("o_q", "o_k", "o_v")[source - 1]][:, off : off + width] = value
-        return put
 
     k0, k1, k2, k3 = blocks, blocks + 1, blocks + 2, blocks + 3
     sent = late_copies(k0, 0)
@@ -453,7 +434,7 @@
     late_form(k0, 0, sent)
     start_sum(k0, sh)
     after_second(last, sh)
-    after_third(last - 1, sh, put_hidden)
+    after_third(last - 1, sh)
 
     def mixer_copy():
         return remote(PS.at[o], PR.at[k1 % 2], pair_s.at[k1 % 2, 0], pair_r.at[k1 % 2, 0], dev_c)
@@ -475,7 +456,7 @@
         form(k1, part, sp, PS.at[c, part][...])
     start_sum(k1, sp)
     after_first(k0, sh)
-    after_third(last, sh, put_hidden)
+    after_third(last, sh)
 
     sent = late_copies(k2, 2)
     for copy in sent:
@@ -505,14 +486,14 @@
         w = grad * NP[0:1, :]
         mean_w = jnp.mean(w, axis=1, keepdims=True)
         mean_wt = jnp.mean(w * t, axis=1, keepdims=True)
-        F3[rows, :] = F3[rows, :] + ST[rows, 0:1] * (w - mean_w - t * mean_wt)
+        Y[rows, :] = (F3[rows, :] + ST[rows, 0:1] * (w - mean_w - t * mean_wt)).astype(bf16)
         NG[0] += fold_rows(grad * t)
         NG[1] += fold_rows(grad)
         return carry
 
     lax.fori_loop(0, T // step_rows, norm_in_back, 0)
-    tok_local = pltpu.make_async_copy(F3.at[:, own_half], ref["o_tok"].at[my_rows, :], local_sem.at[13])
-    tok_cross = remote(F3.at[:, other_half], ref["o_tok"].at[my_rows, :], end_s.at[1], end_r.at[1], dev_c)
+    tok_local = pltpu.make_async_copy(Y.at[:, own_half], ref["o_tok"].at[my_rows, :], local_sem.at[13])
+    tok_cross = remote(Y.at[:, other_half], ref["o_tok"].at[my_rows, :], end_s.at[1], end_r.at[1], dev_c)
     tok_local.start()
     tok_cross.start()
 
@@ -524,22 +505,18 @@
     copy.wait()
     NR[1] = NV[:, own_half] + NR[0]
     if fused:
-        def put_pair(k, part, total):
-            cols = slice(part * COLS, (part + 1) * COLS)
-            ref["o_pair"][:, cols] = total * jnp.exp(ref["PBO"][:, cols])
-
         copy = remote(NR.at[1], NR.at[2], norm_s.at[1], norm_r.at[1], dev_x)
         copy.start()
         after_first(k2, sh)
         after_second(k1, sp)
-        after_third(k0, sh, put_late(0))
+        after_third(k0, sh)
         copy.wait()
         NR[3] = NR[1] + NR[2]
         copy = remote(NR.at[3], NR.at[4], norm_s.at[2], norm_r.at[2], dev_y)
         copy.start()
         after_first(k3, sh)
         after_second(k2, sh)
-        after_third(k1, sp, put_pair)
+        after_third(k1, sp)
         copy.wait()
         total = NR[3] + NR[4]
         NZS[mz] = total
@@ -550,15 +527,17 @@
         for copy in copies:
             copy.start()
         after_second(k3, sh)
-        after_third(k2, sh, put_late(2))
+        after_third(k2, sh)
         for copy in copies:
             copy.wait()
         total = NZS[0]
         for j in range(1, nz):
             total = total + NZS[j]
-        for i, name in enumerate(("o_gi", "o_si", "o_gm", "o_sm")):
-            ref[name][...] = total[i : i + 1, :]
-        after_third(k3, sh, put_late(4))
+        ref["o_norm"][...] = total
+        after_third(k3, sh)
+        for k in range(blocks + 4):
+            for part in range(2):
+                fin_copy(k, part, sp if k == k1 else sh).wait()
     else:
         ref["o_norm"][...] = NR[1]
         for k in (k2, k3):
@@ -567,6 +546,94 @@
     blk_cross.wait()
     tok_local.wait()
     tok_cross.wait()
+
+
+def late_pieces(half, part_no):
+    found, at = [], part_no * COLS
+    while at < (part_no + 1) * COLS:
+        width = min(half - at % half, (part_no + 1) * COLS - at)
+        found.append((at // half, at % half, width, at - part_no * COLS))
+        at += width
+    return found
+
+
+def unpack_kernel(sh, blocks, half, pieces_in, names, *all_refs):
+    ref = dict(zip(names, all_refs))
+    step = ref["tok_in"].shape[0] // pieces_in
+    load_b = pltpu.make_async_copy(ref["o_blk"], ref["blk"], ref["sem"].at[0, 0])
+    save_b = pltpu.make_async_copy(ref["blk"], ref["r_blk"], ref["sem"].at[1, 0])
+    loads, saves = [], []
+    for i in range(pieces_in):
+        rows = slice(i * step, (i + 1) * step)
+        loads.append(pltpu.make_async_copy(ref["o_tok"].at[rows, :], ref["tok_in"].at[rows, :], ref["sem"].at[0, 1 + i]))
+        saves.append(pltpu.make_async_copy(ref["tok_out"].at[rows, :], ref["r_tok"].at[rows, :], ref["sem"].at[1, 1 + i]))
+    load_f = pltpu.make_async_copy(ref["o_fin"], ref["fin"], ref["sem"].at[0, 1 + pieces_in])
+    load_n = pltpu.make_async_copy(ref["o_norm"], ref["norm"], ref["sem"].at[1, 1 + pieces_in])
+    loads[0].start()
+    load_b.start()
+    for load in loads[1:]:
+        load.start()
+    load_f.start()
+    load_n.start()
+    fin, norm = ref["fin"], ref["norm"]
+    for i in range(pieces_in):
+        loads[i].wait()
+        rows = slice(i * step, (i + 1) * step)
+        ref["tok_out"][rows, :] = ref["tok_in"][rows, :].astype(f32)
+        saves[i].start()
+        if i == 0:
+            load_b.wait()
+            save_b.start()
+    load_n.wait()
+    for i, name in enumerate(("r_gi", "r_si", "r_gm", "r_sm")):
+        ref[name][...] = norm[i, :]
+    load_f.wait()
+    for k in range(blocks):
+        cols = slice(k * COLS, (k + 1) * COLS)
+        ref["r_up"][:, cols] = fin[k, 0, 0:sh, :]
+        ref["r_dn"][:, cols] = fin[k, 1, 0:sh, :]
+    for part in range(2):
+        ref["r_pair"][:, part * COLS : (part + 1) * COLS] = fin[blocks + 1, part]
+    for k, first_part in ((blocks, 0), (blocks + 2, 2), (blocks + 3, 4)):
+        for part in range(2):
+            for source, off, width, at in late_pieces(half, first_part + part):
+                value = fin[k, part, 0:sh, at : at + width]
+                ref[("r_wo", "r_q", "r_k", "r_v")[source]][:, off : off + width] = value
+    for save in saves:
+        save.wait()
+    save_b.wait()
+
+
+def unpack(T, D, FH, sh, sp, out):
+    half = D // 2
+    blocks = FH // COLS
+    pieces_in = 4
+    any_spec, vmem = pl.BlockSpec(memory_space=pl.ANY), pl.BlockSpec(memory_space=pltpu.VMEM)
+    inputs = {"o_blk": any_spec, "o_tok": any_spec, "o_norm": any_spec, "o_fin": any_spec}
+    results = {"r_blk": (any_spec, (2 * T, half), bf16), "r_tok": (any_spec, (2 * T, half), f32)}
+    results |= {name: (vmem, (half,), f32) for name in ("r_gi", "r_si", "r_gm", "r_sm")}
+    results |= {name: (vmem, (sh, half), f32) for name in ("r_q", "r_k", "r_v", "r_wo")}
+    results |= {
+        "r_up": (vmem, (sh, FH), f32), "r_dn": (vmem, (sh, FH), f32),
+        "r_pair": (vmem, (sp, T // 2), f32),
+    }
+    scratch = {
+        "blk": pltpu.VMEM((2 * T, half), bf16), "tok_in": pltpu.VMEM((2 * T, half), bf16),
+        "tok_out": pltpu.VMEM((2 * T, half), f32), "sem": pltpu.SemaphoreType.DMA((2, 2 + pieces_in)),
+        "fin": pltpu.VMEM(out["o_fin"].shape, f32), "norm": pltpu.VMEM((8, half), f32),
+    }
+    names = tuple(inputs) + tuple(results) + tuple(scratch)
+    values = pl.pallas_call(
+        functools.partial(unpack_kernel, sh, blocks, half, pieces_in, names),
+        out_shape=tuple(jax.ShapeDtypeStruct(shape, kind) for _, shape, kind in results.values()),
+        in_specs=list(inputs.values()),
+        out_specs=tuple(spec for spec, _, _ in results.values()),
+        scratch_shapes=list(scratch.values()),
+        compiler_params=pltpu.CompilerParams(vmem_limit_bytes=63 << 20),
+    )(*(out[name] for name in inputs))
+    done = {"o_" + name[2:]: value for name, value in zip(results, values)}
+    done["o_wo"], done["o_dn"] = done["o_wo"].T, done["o_dn"].T
+    return done
 
 
 def run_block(T, D, FH, R, args):
@@ -582,18 +649,13 @@
         "wv": any_spec, "wo": any_spec, "gm": vmem, "sm": vmem, "wu": any_spec, "wd": any_spec,
         "pair_bias": any_spec, "out_grad": any_spec,
     }
-    outputs = {"o_blk": (any_spec, (2 * T, half), bf16), "o_tok": (any_spec, (2 * T, half), f32)}
+    outputs = {
+        "o_blk": (any_spec, (2 * T, half), bf16), "o_tok": (any_spec, (2 * T, half), bf16),
+        "o_norm": (vmem, (8, half), f32),
+    }
     if fused:
-        for name in ("o_gi", "o_si", "o_gm", "o_sm"):
-            outputs[name] = (vmem, (1, half), f32)
-        for name in ("o_q", "o_k", "o_v"):
-            outputs[name] = (vmem, (sh, half), f32)
-        outputs["o_wo"] = (vmem, (half, sh), f32)
-        outputs["o_up"] = (vmem, (sh, FH), f32)
-        outputs["o_dn"] = (vmem, (FH, sh), f32)
-        outputs["o_pair"] = (vmem, (sp, T // 2), f32)
+        outputs["o_fin"] = (any_spec, (blocks + 4, 2, sp, COLS), f32)
     else:
-        outputs["o_norm"] = (vmem, (8, half), f32)
         outputs["GO"] = (any_spec, (blocks + 4, 2, nb, sp, COLS), bf16)
     wide = (T, D)
     scratch = {name: pltpu.VMEM(wide, bf16) for name in ("XB", "OG", "HN", "G", "Y", "QQ", "RT", "RZ", "T2")}
@@ -611,6 +673,8 @@
         "R3": pltpu.VMEM((SLOTS, 2, nz - 1, sp, COLS), bf16) if fused else pltpu.VMEM((8, TILE), f32),
         "NG": pltpu.VMEM((4, 8, D), f32), "NV": pltpu.VMEM((8, D), f32), "NR": pltpu.VMEM((5, 8, half), f32),
         "NZS": pltpu.VMEM((nz, 8, half), f32), "PBO": pltpu.VMEM((sp, T // 2), f32),
+        "FIN": pltpu.VMEM((blocks + 4, 2, sp, COLS), f32) if fused else pltpu.VMEM((8, TILE), f32),
+        "fin_sem": pltpu.SemaphoreType.DMA((blocks + 4, 2)),
         "local_sem": pltpu.SemaphoreType.DMA((16,)),
         "entry_s": pltpu.SemaphoreType.DMA((16,)), "entry_r": pltpu.SemaphoreType.DMA((16,)),
         "pair_s": pltpu.SemaphoreType.DMA((2, 5)), "pair_r": pltpu.SemaphoreType.DMA((2, 5)),
@@ -631,7 +695,8 @@
     )(*args)
     out = dict(zip(outputs, results))
     if fused:
-        return out
+        return unpack(T, D, FH, sh, sp, out)
+    out["o_tok"] = out["o_tok"].astype(f32)
     parts = out.pop("GO")
     height = lambda v, rows: v.reshape(nb, sp, v.shape[-1])[:, : rows // nb].reshape(rows, v.shape[-1])
     join = lambda chosen: jnp.concatenate(chosen, 1).astype(f32)
@@ -648,7 +713,7 @@
     out["o_pair"] = pair * jnp.exp(bias)
     norms = lax.psum(out["o_norm"], "rows")
     for i, name in enumerate(("o_gi", "o_si", "o_gm", "o_sm")):
-        out[name] = norms[i : i + 1]
+        out[name] = norms[i]
     return out
 
 
@@ -659,16 +724,13 @@
     T = segments.shape[1]
     D, FH = up_weight.shape
     R = lax.axis_size("rows")
-    row = lambda v: v.reshape(1, v.shape[0])
     out = run_block(T, D, FH, R, (
-        tokens, segments, row(gain_in), row(shift_in), query_weight, key_weight, value_weight, out_weight,
-        row(gain_mid), row(shift_mid), up_weight, down_weight, pair_bias, out_grad,
+        tokens, segments, gain_in, shift_in, query_weight, key_weight, value_weight, out_weight,
+        gain_mid, shift_mid, up_weight, down_weight, pair_bias, out_grad,
     ))
-    flat = lambda name: out[name].reshape(out[name].shape[1])
-    return (
-        out["o_blk"], out["o_tok"], flat("o_gi"), flat("o_si"), out["o_q"], out["o_k"], out["o_v"], out["o_wo"],
-        flat("o_gm"), flat("o_sm"), out["o_up"], out["o_dn"], out["o_pair"],
-    )
+    return tuple(out[name] for name in (
+        "o_blk", "o_tok", "o_gi", "o_si", "o_q", "o_k", "o_v", "o_wo", "o_gm", "o_sm", "o_up", "o_dn", "o_pair",
+    ))
 
 
 def solution(mesh):

time: 145 us -> 128 us (0.88)
  local copies, waits for them, and re-layouts: 16.4 us -> 0 us
  other arithmetic: 5.1 us -> 0 us
  Pallas kernels: 123 us -> 127 us
    unnamed x21 -> x0, local copies, waits for them, and re-layouts: 11.4 us -> none
    pallas_call x4 -> x0, other arithmetic: 5.1 us -> none  [run_block(): pl.pallas_call(functools.partial(block_kernel, T, D, FH, R, fused, names)...]
    reshape x4 -> x0, local copies, waits for them, and re-layouts: 4.98 us -> none  [on_device(): row = lambda v: v.reshape(1, v.shape[0])]
    pallas_call x0 -> x1, Pallas kernels: none -> 4.53 us  [unpack(): pl.pallas_call(functools.partial(unpack_kernel, sh, blocks, half, pieces_...]
where the time goes in v2:
time: 128 us
  Pallas kernels  127 us (99%)
    pallas_call x1, Pallas kernels, run_block(): pl.pallas_call(functools.partial(block_kernel, T, D, FH, R, fused, names)...  123 us
    pallas_call x1, Pallas kernels, unpack(): pl.pallas_call(functools.partial(unpack_kernel, sh, blocks, half, pieces_...  4.53 us

profile of v2, /device:TPU:0, one launch (start us, length us, event | category | flops | bytes accessed | tf_op | source)
XLA Modules:
  0.0 128.2 jit_solution(17540940086650311412)
XLA Ops:
  0.7 122.8 %shard_map.237 = (bf16[2048,384]{1,0:T(8,128)(2,1)}, bf16[2048,384]{1,0:T(8,128)(2,1)}, f32[8,384]{1,0:T(8,128)}, f32[10,2,64,256]{3,2,1,0:T(8,128)}) custom-call(bf16[2048,384]{1,0:T(8,128)(2,1)} %all_refs_0_.1, s32[2,1024]{1,0:T(2,128)} %all_refs_1_.1, f32[384]{0:T(512)} %all_refs_2_.1, f32[384]{0:T(512)} %all_refs_3_.1, bf16[768,384]{1,0:T(8,128)(2,1)} %all_refs_4_.1, ...), custom_call_target="tpu_custom_call" | custom-call | tf_op jit(solution)/shard_map/pallas_call | solution.py:686
  123.4 4.5 %shard_map.238 = (bf16[2048,384]{1,0:T(8,128)(2,1)}, f32[2048,384]{1,0:T(8,128)}, f32[384]{0:T(512)}, f32[384]{0:T(512)}, f32[384]{0:T(512)}, /*index=5*/f32[384...) custom-call(bf16[2048,384]{1,0:T(8,128)(2,1)} %get-tuple-element.30., ...), custom_call_target="tpu_custom_call" | custom-call | tf_op jit(solution)/shard_map/pallas_call | solution.py:626

commit v3 on v2

v3 whole, which is shorter than its diff:
```python
import functools
from types import SimpleNamespace

import jax
import jax.numpy as jnp
from jax import lax
from jax.experimental import pallas as pl
from jax.experimental.pallas import tpu as pltpu
from jax.sharding import PartitionSpec as P

MESH = pl.DeviceIdType.MESH
ANY, VMEM = pl.BlockSpec(memory_space=pl.ANY), pl.BlockSpec(memory_space=pltpu.VMEM)
WIN = 256
EPSILON = 1e-05
TILE = 128
COLS = 256
SLOTS = 4
STEP = 256
f32 = jnp.float32
bf16 = jnp.bfloat16


def dot(left, right, cl=1, cr=0):
    return lax.dot_general(left, right, (((cl,), (cr,)), ((), ())), preferred_element_type=f32)


def dot_nt(left, right):
    return dot(left, right, 1, 1)


def dot_tn(left, right):
    return dot(left, right, 0, 0)


def gelu_pair(p):
    phi = 0.5 * (1.0 + lax.erf(p * 0.7071067811865476))
    return p * phi, phi + p * (jnp.exp(-0.5 * p * p) * 0.3989422804014327)


def fold_rows(v):
    return jnp.sum(v.reshape(v.shape[0] // 8, 8, v.shape[1]), axis=0)


def late_pieces(half, part_no):
    found, at = [], part_no * COLS
    while at < (part_no + 1) * COLS:
        width = min(half - at % half, (part_no + 1) * COLS - at)
        found.append((at // half, at % half, width, at - part_no * COLS))
        at += width
    return found


def block_kernel(T, D, FH, R, fused, names, *all_refs):
    ref = SimpleNamespace(**dict(zip(names, all_refs)))
    half = D // 2
    blocks = FH // COLS
    nb = R if fused else 16
    nz = nb // 4
    sh, sp = D // nb, T // nb
    r = lax.axis_index("rows")
    c = lax.axis_index("chan")
    o = 1 - c
    mx, my, mz = lax.rem(r, 2), lax.rem(r // 2, 2), r // 4
    z0, z1 = lax.rem(mz, 2), mz // 2
    dev_c = (r, o)
    dev_x = (r + 1 - 2 * mx, c)
    dev_y = (r + 2 - 4 * my, c)
    dev_z = [(lax.rem(mz + j, nz) * 4 + lax.rem(r, 4), c) for j in range(1, nz)]
    dev_z0 = (r + 4 - 8 * z0, c)
    dev_z1 = (r + 8 - 16 * z1, c)
    own_half = pl.ds(pl.multiple_of(c * half, TILE), half)
    other_half = pl.ds(pl.multiple_of(o * half, TILE), half)

    XB, OG, HN, G = ref.XB, ref.OG, ref.HN, ref.G
    Y, QQ, RT, RZ, T2 = ref.Y, ref.QQ, ref.RT, ref.RZ, ref.T2
    AB, MM, F1, F3, ST = ref.AB, ref.MM, ref.F1, ref.F3, ref.ST
    WQ, WK, WV, WO, WU, WD = ref.WQ, ref.WK, ref.WV, ref.WO, ref.WU, ref.WD
    SD, SC, NP, NPS, NPR = ref.SD, ref.SC, ref.NP, ref.NPS, ref.NPR
    PS, PR, S, RX, FIN = ref.PS, ref.PR, ref.S, ref.RX, ref.FIN
    NG, NV, NR, NZS = ref.NG, ref.NV, ref.NR, ref.NZS

    def remote(src, dst, send, recv, device):
        return pltpu.make_async_remote_copy(
            src_ref=src, dst_ref=dst, send_sem=send, recv_sem=recv, device_id=device, device_id_type=MESH
        )

    my_rows, other_rows = pl.ds(c * T, T), pl.ds(o * T, T)
    h2 = T // 2
    local, cross = [], []

    def load(src, dst, away=None, there=None):
        at = len(local)
        local.append(pltpu.make_async_copy(src, dst, ref.local_sem.at[at]))
        cross.append(None if away is None else remote(away, there, ref.entry_s.at[at], ref.entry_r.at[at], dev_c))
        local[at].start()
        return at

    bias_at = [
        load(ref.pair_bias.at[0:h2, 0:D], F3.at[0:h2, :]),
        load(ref.pair_bias.at[h2:T, T - D : T], F3.at[h2:T, :]),
    ]
    tokens_at = load(
        ref.tokens.at[my_rows, :], XB.at[:, own_half], ref.tokens.at[other_rows, :], XB.at[:, own_half]
    )
    qkv_at = [
        load(src, dst.at[:, 0:half], src, dst.at[:, half:D]) for src, dst in ((ref.wk, WK), (ref.wv, WV), (ref.wq, WQ))
    ]
    wo_at = load(ref.wo, WO.at[0:half, :], ref.wo, WO.at[half:D, :])
    og_at = load(
        ref.out_grad.at[my_rows, :], OG.at[:, own_half], ref.out_grad.at[other_rows, :], OG.at[:, own_half]
    )
    wide = 2 * COLS

    def up_piece(i, away):
        cols = pl.ds(pl.multiple_of(i * wide, wide), wide)
        if away:
            return remote(ref.wu.at[:, cols], WU.at[D : 2 * D, cols], ref.up_s.at[i], ref.up_r.at[i], dev_c)
        return pltpu.make_async_copy(ref.wu.at[:, cols], WU.at[0:D, cols], ref.up_l.at[i])

    def down_piece(i, away):
        src = ref.wd.at[pl.ds(pl.multiple_of(i * wide, wide), wide), :]
        if away:
            dst = WD.at[pl.ds(pl.multiple_of(FH + i * wide, wide), wide), :]
            return remote(src, dst, ref.down_s.at[i], ref.down_r.at[i], dev_c)
        return pltpu.make_async_copy(src, WD.at[pl.ds(pl.multiple_of(i * wide, wide), wide), :], ref.down_l.at[i])

    pbo_at = None
    if fused:
        pair_rows = pl.ds(pl.multiple_of(r * sp, 8), sp)
        pair_cols = pl.ds(pl.multiple_of(c * (T // 2), TILE), T // 2)
        pbo_at = load(ref.pair_bias.at[pair_rows, pair_cols], ref.PBO)
    for i in range(blocks // 2):
        up_piece(i, False).start()
        down_piece(i, False).start()

    NPS[...] = jnp.zeros(NPS.shape, f32)
    for i, vector in enumerate((ref.gi, ref.si, ref.gm, ref.sm)):
        NPS[i : i + 1, :] = vector[...].reshape(1, half)
    norms_cross = remote(NPS, NPR, ref.entry_s.at[15], ref.entry_r.at[15], dev_c)
    barrier = pltpu.get_barrier_semaphore()
    greeted = [dev_c] + ([dev_x, dev_y] + dev_z if fused else [])
    for device in greeted:
        pl.semaphore_signal(barrier, inc=1, device_id=device, device_id_type=MESH)
    pl.semaphore_wait(barrier, len(greeted))
    norms_cross.start()
    for at in [tokens_at] + qkv_at:
        cross[at].start()

    def ready(*chosen):
        for at in chosen:
            local[at].wait()
            if cross[at] is not None:
                cross[at].wait()

    seg = ref.segments[pl.ds(c, 1), :].astype(f32)
    SC[...] = jnp.broadcast_to(seg, (TILE, T)).T
    ready(*bias_at)
    row_id = lax.broadcasted_iota(jnp.int32, (TILE, TILE), 0)
    col_id = lax.broadcasted_iota(jnp.int32, (TILE, TILE), 1)
    for a in range(T // TILE):
        rows = slice(a * TILE, (a + 1) * TILE)
        shift = 0 if a * TILE < h2 else T - D
        for b in range(T // TILE):
            cols = slice(b * TILE, (b + 1) * TILE)
            far = abs(a - b) * TILE
            if far - TILE + 1 >= T // 2:
                MM[rows, cols] = jnp.zeros((TILE, TILE), bf16)
                continue
            same = SC[rows, :] == seg[:, cols]
            if far - TILE + 1 >= WIN:
                weight = jnp.ones((TILE, TILE), f32)
            else:
                weight = jnp.exp(F3[rows, b * TILE - shift : (b + 1) * TILE - shift])
                if far + TILE - 1 >= WIN:
                    inside = jnp.abs(row_id - col_id + (a - b) * TILE) < WIN
                    weight = jnp.where(inside, weight, 1.0)
            MM[rows, cols] = jnp.where(same, weight, 0.0).astype(bf16)

    norms_cross.wait()
    for i in range(4):
        NP[i : i + 1, own_half] = NPS[i : i + 1, :]
        NP[i : i + 1, other_half] = NPR[i : i + 1, :]
    ready(tokens_at)

    def norm_in(i, carry):
        rows = pl.ds(i * STEP, STEP)
        x = XB[rows, :].astype(f32)
        centred = x - jnp.mean(x, axis=1, keepdims=True)
        inv = lax.rsqrt(jnp.mean(centred * centred, axis=1, keepdims=True) + EPSILON)
        t = centred * inv
        F1[rows, :] = x
        XB[rows, :] = t.astype(bf16)
        HN[rows, :] = (t * NP[0:1, :] + NP[1:2, :]).astype(bf16)
        ST[rows, 0:1] = inv
        return carry

    lax.fori_loop(0, T // STEP, norm_in, 0)
    cross[wo_at].start()
    cross[og_at].start()
    for i in range(blocks // 2):
        up_piece(i, True).start()
        down_piece(i, True).start()
    for at in qkv_at:
        local[at].wait()

    for j in range(D // COLS):
        if j * COLS <= half < (j + 1) * COLS:
            for at in qkv_at:
                cross[at].wait()
        cols = slice(j * COLS, (j + 1) * COLS)
        late = slice(D + j * COLS, D + (j + 1) * COLS)
        e = jnp.exp(dot(HN[...], WK[:, cols]))
        a = (e * dot(HN[...], WV[:, cols])).astype(bf16)
        AB[:, cols] = a
        AB[:, late] = e.astype(bf16)
        gate = jax.nn.sigmoid(dot(HN[...], WQ[:, cols]))
        inv = 1.0 / dot(MM[...], AB[:, late])
        ratio = dot(MM[...], AB[:, cols]) * inv
        y = gate * ratio
        Y[:, cols] = y.astype(bf16)
        QQ[:, cols] = (y * (1.0 - gate)).astype(bf16)
        RT[:, cols] = ratio.astype(bf16)
        RZ[:, cols] = (gate * inv).astype(bf16)

    ready(wo_at)
    F1[...] += dot(Y[...], WO[...])

    def norm_mid(i, carry):
        rows = pl.ds(i * STEP, STEP)
        x = F1[rows, :]
        centred = x - jnp.mean(x, axis=1, keepdims=True)
        inv = lax.rsqrt(jnp.mean(centred * centred, axis=1, keepdims=True) + EPSILON)
        t = centred * inv
        T2[rows, :] = t.astype(bf16)
        G[rows, :] = (t * NP[2:3, :] + NP[3:4, :]).astype(bf16)
        ST[rows, 1:2] = inv
        F3[rows, :] = jnp.zeros((STEP, D), f32)
        return carry

    lax.fori_loop(0, T // STEP, norm_mid, 0)
    ready(og_at)
    if fused:
        ready(pbo_at)

    axes = (((mx, dev_x), (my, dev_y)), ((my, dev_y), (mx, dev_x)))
    room = (0, nb // 2, nb // 2 + nb // 4)

    def place(b, part):
        if not fused:
            return b
        bx, by, bz = b % 2, (b // 2) % 2, b // 4
        outer, inner = (bx, by) if part == 0 else (by, bx)
        return (outer * 2 + inner) * nz + bz

    def chunk(k, height=sh, reach=None):
        return SimpleNamespace(k=k, height=height, reach=reach, slot=k % SLOTS)

    def form(ch, part, own, at=0):
        width, height = own.shape[1], ch.height
        for b in range(nb):
            rows = slice(b * height, (b + 1) * height)
            total = own[rows, :].astype(bf16) + PR[ch.k % 2, part, rows, at : at + width]
            S[ch.slot, part, place(b, part), 0:height, at : at + width] = total

    def span(part, n):
        base, size = 0, nb
        for bit, _ in axes[part][: n - 1]:
            size //= 2
            base = base + bit * size
        return base, size

    def runs(ch, part, base, size):
        if ch.reach is None:
            return [(base, 0, size)]
        low, count = ch.reach[part]
        return [(base + i * nz + low, i * count, count) for i in range(size // nz)]

    def stage(ch, part, n):
        rows, copies = pl.ds(0, ch.height), []
        base, size = span(part, n)
        if n < 3:
            bit, device = axes[part][n - 1]
            for i, (start, at, count) in enumerate(runs(ch, part, base + (1 - bit) * (size // 2), size // 2)):
                sem = 2 * (n - 1) + i
                copies.append(remote(
                    S.at[ch.slot, part, pl.ds(start, count), rows, :],
                    RX.at[ch.slot, part, pl.ds(room[n - 1] + at, count), rows, :],
                    ref.ring_s.at[ch.slot, part, sem], ref.ring_r.at[ch.slot, part, sem], device,
                ))
        else:
            for j in range(1, nz):
                sem = 2 + j
                copies.append(remote(
                    S.at[ch.slot, part, base + lax.rem(mz + j, nz), rows, :],
                    RX.at[ch.slot, part, room[n - 1] + j - 1, rows, :],
                    ref.ring_s.at[ch.slot, part, sem], ref.ring_r.at[ch.slot, part, sem], dev_z[j - 1],
                ))
        return copies

    def whole(ch):
        return pltpu.make_async_copy(S.at[ch.slot], ref.GO.at[ch.k], ref.ring_s.at[ch.slot, 0, 0])

    def fin_copy(ch, part):
        rows = pl.ds(0, ch.height)
        return pltpu.make_async_copy(
            FIN.at[ch.k, part, rows, :], ref.o_fin.at[ch.k, part, rows, :], ref.fin_sem.at[ch.k, part]
        )

    def launch(ch):
        if not fused:
            whole(ch).start()
            return
        for part in range(2):
            for copy in stage(ch, part, 1):
                copy.start()

    def advance(ch, n):
        if not fused:
            if n == 1:
                whole(ch).wait()
            return
        rows = slice(0, ch.height)
        for part in range(2):
            for copy in stage(ch, part, n):
                copy.wait()
            if n < 3:
                for start, at, count in runs(ch, part, *span(part, n + 1)):
                    S[ch.slot, part, pl.ds(start, count), rows, :] += RX[
                        ch.slot, part, pl.ds(room[n - 1] + at, count), rows, :
                    ]
                for copy in stage(ch, part, n + 1):
                    copy.start()
                continue
            total = S[ch.slot, part, span(part, 3)[0] + mz, rows, :].astype(f32)
            for j in range(nz - 1):
                total = total + RX[ch.slot, part, room[2] + j, rows, :].astype(f32)
            if ch.height != sh:
                total = total * jnp.exp(ref.PBO[:, pl.ds(pl.multiple_of(pair_part[part] * COLS, COLS), COLS)])
            FIN[ch.k, part, rows, :] = total
            fin_copy(ch, part).start()

    def hidden_step(owner, i):
        cols = pl.ds(pl.multiple_of(i * COLS, COLS), COLS)
        up_at = slice(owner * D, (owner + 1) * D)
        down_at = pl.ds(pl.multiple_of(owner * FH + i * COLS, COLS), COLS)
        s, slope = gelu_pair(dot(G[...], WU[up_at, cols]))
        SD[:, 0:COLS] = s.astype(bf16)
        SD[:, COLS:] = (dot_nt(OG[...], WD[down_at, :]) * slope).astype(bf16)
        F1[...] += dot(SD[:, 0:COLS], WD[down_at, :])
        F3[...] += dot_nt(SD[:, COLS:], WU[up_at, cols])
        return dot_tn(G[...], SD[:, COLS:]), dot_tn(OG[...], SD[:, 0:COLS])

    def pair_copy(slot, height):
        return remote(
            PS.at[slot, :, pl.ds(0, height), :], PR.at[slot, :, pl.ds(0, height), :],
            ref.pair_s.at[slot, 0], ref.pair_r.at[slot, 0], dev_c,
        )

    def hidden_pair(i, carry):
        for copies in (up_piece, down_piece):
            copies(i, False).wait()
            copies(i, True).wait()
        for q in range(2):
            ch = chunk(2 * i + q)
            up, down = hidden_step(1, ch.k)
            PS[q, 0, 0:D, :] = up.astype(bf16)
            PS[q, 1, 0:D, :] = down.astype(bf16)
            pair_copy(q, D).start()
            for n in (1, 2, 3):
                before = chunk(2 * i + q - 1 - n)
                pl.when(2 * i + q >= 1 + n)(functools.partial(advance, before, n))
            up, down = hidden_step(0, ch.k)
            pair_copy(q, D).wait()
            form(ch, 0, up)
            form(ch, 1, down)
            launch(ch)
        return carry

    lax.fori_loop(0, blocks // 2, hidden_pair, 0)
    h2, h3, h4, h5 = (chunk(blocks - i) for i in (4, 3, 2, 1))
    k0, k2, k3 = chunk(blocks), chunk(blocks + 2), chunk(blocks + 3)
    pair_part = (c, 1 - c)
    k1 = chunk(blocks + 1, sp, ((2 * c, 2), (c, 3)) if fused else None)

    def finish_out(i, carry):
        rows = pl.ds(i * STEP, STEP)
        G[rows, :] = F1[rows, :].astype(bf16)
        return carry

    lax.fori_loop(0, T // STEP, finish_out, 0)
    blk_local = pltpu.make_async_copy(G.at[:, own_half], ref.o_blk.at[my_rows, :], ref.end_l.at[0])
    blk_cross = remote(G.at[:, other_half], ref.o_blk.at[my_rows, :], ref.end_s.at[0], ref.end_r.at[0], dev_c)
    blk_local.start()
    blk_cross.start()
    advance(h2, 3)
    advance(h3, 2)
    advance(h4, 1)

    NG[...] = jnp.zeros(NG.shape, f32)

    def norm_mid_back(i, carry):
        rows = pl.ds(i * STEP, STEP)
        grad, t = F3[rows, :], T2[rows, :].astype(f32)
        w = grad * NP[2:3, :]
        mean_w = jnp.mean(w, axis=1, keepdims=True)
        mean_wt = jnp.mean(w * t, axis=1, keepdims=True)
        dx = OG[rows, :].astype(f32) + ST[rows, 1:2] * (w - mean_w - t * mean_wt)
        F3[rows, :] = dx
        T2[rows, :] = dx.astype(bf16)
        NG[2] += fold_rows(grad * t)
        NG[3] += fold_rows(grad)
        return carry

    lax.fori_loop(0, T // STEP, norm_mid_back, 0)

    NZ = WU
    for j in range(D // COLS):
        cols = slice(j * COLS, (j + 1) * COLS)
        late = slice(D + j * COLS, D + (j + 1) * COLS)
        dm = dot_nt(T2[...], WO[cols, :])
        WD[0:T, cols] = (dm * QQ[:, cols].astype(f32)).astype(bf16)
        dn = dm * RZ[:, cols].astype(f32)
        NZ[0:T, cols] = dn.astype(bf16)
        NZ[0:T, late] = (-dn * RT[:, cols].astype(f32)).astype(bf16)
    OG[0:D, :] = dot_tn(T2[...], Y[...]).astype(bf16)
    advance(h3, 3)
    advance(h4, 2)
    advance(h5, 1)
    QQ[0:D, :] = dot_tn(HN[...], WD[0:T, :]).astype(bf16)

    sources = (OG, QQ, RZ, RT)
    pieces = functools.partial(late_pieces, half)

    def late_copies(ch, first_part):
        slot, copies = ch.k % 2, []
        for part in range(2):
            for source, off, width, at in pieces(first_part + part):
                cols = slice(half + off, half + off + width)
                copies.append(remote(
                    sources[source].at[pl.ds(0, D), cols], PR.at[slot, part, pl.ds(0, D), pl.ds(at, width)],
                    ref.pair_s.at[slot, 1 + len(copies)], ref.pair_r.at[slot, 1 + len(copies)], dev_c,
                ))
        for copy in copies:
            copy.start()
        return copies

    def late_form(ch, first_part, copies):
        for copy in copies:
            copy.wait()
        for part in range(2):
            for source, off, width, at in pieces(first_part + part):
                form(ch, part, sources[source][0:D, off : off + width], at)

    sent = late_copies(k0, 0)

    def mixer_grad(j):
        cols = slice(j * COLS, (j + 1) * COLS)
        low, high = max(0, (j - 1) * COLS), min(T, (j + 2) * COLS)
        target = PS.at[j // 2, (j % 2) if j < 2 else 1 - j % 2]
        for start, stop in ((0, low), (high, T)):
            if stop > start:
                target[start:stop, :] = jnp.zeros((stop - start, COLS), bf16)
        grad = dot_nt(NZ[low:high, :], AB[cols, :])
        for t in range(COLS // TILE):
            at = j * COLS + t * TILE
            same = SC[low:high, :] == seg[:, at : at + TILE]
            gap = (
                lax.broadcasted_iota(jnp.int32, (high - low, TILE), 0)
                - lax.broadcasted_iota(jnp.int32, (high - low, TILE), 1)
                + (low - at)
            )
            kept = jnp.where(same & (jnp.abs(gap) < WIN), grad[:, t * TILE : (t + 1) * TILE], 0.0)
            target[low:high, t * TILE : (t + 1) * TILE] = kept.astype(bf16)

    mixer_grad(0)
    mixer_grad(1)
    late_form(k0, 0, sent)
    launch(k0)
    mixer_grad(2)
    mixer_grad(3)
    mixer_copy = remote(PS.at[o], PR.at[k1.k % 2], ref.pair_s.at[k1.k % 2, 0], ref.pair_r.at[k1.k % 2, 0], dev_c)
    mixer_copy.start()

    def mixing_back(j):
        cols = slice(j * COLS, (j + 1) * COLS)
        late = slice(D + j * COLS, D + (j + 1) * COLS)
        da = dot_tn(MM[...], NZ[0:T, cols])
        db = dot_tn(MM[...], NZ[0:T, late])
        e = AB[:, late].astype(f32)
        WD[T : 2 * T, cols] = (db * e + da * AB[:, cols].astype(f32)).astype(bf16)
        WD[2 * T : 3 * T, cols] = (da * e).astype(bf16)

    advance(h5, 2)
    mixing_back(0)
    mixer_copy.wait()
    for part in range(2):
        form(k1, part, PS.at[c, part][...])
    launch(k1)
    advance(h4, 3)
    mixing_back(1)
    advance(k0, 1)
    mixing_back(2)
    RZ[0:D, :] = dot_tn(HN[...], WD[T : 2 * T, :]).astype(bf16)
    sent = late_copies(k2, 2)
    advance(h5, 3)
    RT[0:D, :] = dot_tn(HN[...], WD[2 * T : 3 * T, :]).astype(bf16)
    late_form(k2, 2, sent)
    launch(k2)
    sent = late_copies(k3, 4)

    for j in range(D // COLS):
        cols = slice(j * COLS, (j + 1) * COLS)
        F1[:, cols] = (
            dot_nt(WD[0:T, :], WQ[cols, :])
            + dot_nt(WD[T : 2 * T, :], WK[cols, :])
            + dot_nt(WD[2 * T : 3 * T, :], WV[cols, :])
        )
        if j == 0:
            advance(k1, 1)
            late_form(k3, 4, sent)
            launch(k3)
            advance(k0, 2)
    advance(k2, 1)
    advance(k1, 2)
    advance(k0, 3)

    def norm_in_back(i, carry):
        rows = pl.ds(i * STEP, STEP)
        grad, t = F1[rows, :], XB[rows, :].astype(f32)
        w = grad * NP[0:1, :]
        mean_w = jnp.mean(w, axis=1, keepdims=True)
        mean_wt = jnp.mean(w * t, axis=1, keepdims=True)
        Y[rows, :] = (F3[rows, :] + ST[rows, 0:1] * (w - mean_w - t * mean_wt)).astype(bf16)
        NG[0] += fold_rows(grad * t)
        NG[1] += fold_rows(grad)
        return carry

    lax.fori_loop(0, T // STEP, norm_in_back, 0)
    tok_local = pltpu.make_async_copy(Y.at[:, own_half], ref.o_tok.at[my_rows, :], ref.end_l.at[1])
    tok_cross = remote(Y.at[:, other_half], ref.o_tok.at[my_rows, :], ref.end_s.at[1], ref.end_r.at[1], dev_c)
    tok_local.start()
    tok_cross.start()

    NV[...] = jnp.zeros(NV.shape, f32)
    for i in range(4):
        NV[i : i + 1, :] = jnp.sum(NG[i], axis=0, keepdims=True)
    copy = remote(NV.at[:, other_half], NR.at[0], ref.norm_s.at[0], ref.norm_r.at[0], dev_c)
    copy.start()
    copy.wait()
    NR[1] = NV[:, own_half] + NR[0]
    if fused:
        copy = remote(NR.at[1], NR.at[2], ref.norm_s.at[1], ref.norm_r.at[1], dev_x)
        copy.start()
        advance(k3, 1)
        advance(k2, 2)
        copy.wait()
        NR[3] = NR[1] + NR[2]
        copy = remote(NR.at[3], NR.at[4], ref.norm_s.at[2], ref.norm_r.at[2], dev_y)
        copy.start()
        advance(k1, 3)
        advance(k3, 2)
        copy.wait()
        NZS[mz] = NR[3] + NR[4]
        copies = [
            remote(NZS.at[mz], NZS.at[mz], ref.norm_s.at[2 + j], ref.norm_r.at[2 + j], dev_z[j - 1])
            for j in range(1, nz)
        ]
        for copy in copies:
            copy.start()
        advance(k2, 3)
        advance(k3, 3)
        for copy in copies:
            copy.wait()
        total = NZS[0]
        for j in range(1, nz):
            total = total + NZS[j]
        ref.o_norm[...] = total
        for k in range(blocks + 4):
            for part in range(2):
                fin_copy(k1 if k == k1.k else chunk(k), part).wait()
    else:
        ref.o_norm[...] = NR[1]
        advance(k3, 1)
    blk_local.wait()
    blk_cross.wait()
    tok_local.wait()
    tok_cross.wait()


def unpack_kernel(sh, blocks, half, count, names, *all_refs):
    ref = SimpleNamespace(**dict(zip(names, all_refs)))
    step = ref.tok_in.shape[0] // count
    load_b = pltpu.make_async_copy(ref.o_blk, ref.blk, ref.sem.at[0, 0])
    save_b = pltpu.make_async_copy(ref.blk, ref.r_blk, ref.sem.at[1, 0])
    loads, saves = [], []
    for i in range(count):
        rows = slice(i * step, (i + 1) * step)
        loads.append(pltpu.make_async_copy(ref.o_tok.at[rows, :], ref.tok_in.at[rows, :], ref.sem.at[0, 1 + i]))
        saves.append(pltpu.make_async_copy(ref.tok_out.at[rows, :], ref.r_tok.at[rows, :], ref.sem.at[1, 1 + i]))
    load_f = pltpu.make_async_copy(ref.o_fin, ref.fin, ref.sem.at[0, 1 + count])
    load_n = pltpu.make_async_copy(ref.o_norm, ref.norm, ref.sem.at[1, 1 + count])
    loads[0].start()
    load_b.start()
    for load in loads[1:]:
        load.start()
    load_f.start()
    load_n.start()
    fin, norm = ref.fin, ref.norm
    for i in range(count):
        loads[i].wait()
        rows = slice(i * step, (i + 1) * step)
        ref.tok_out[rows, :] = ref.tok_in[rows, :].astype(f32)
        saves[i].start()
        if i == 0:
            load_b.wait()
            save_b.start()
    load_n.wait()
    for i, vector in enumerate((ref.r_gi, ref.r_si, ref.r_gm, ref.r_sm)):
        vector[...] = norm[i, :]
    load_f.wait()
    for k in range(blocks):
        cols = slice(k * COLS, (k + 1) * COLS)
        ref.r_up[:, cols] = fin[k, 0, 0:sh, :]
        ref.r_dn[:, cols] = fin[k, 1, 0:sh, :]
    low, high = fin[blocks + 1, 0], fin[blocks + 1, 1]
    first = lax.axis_index("chan") == 0
    ref.r_pair[:, 0:COLS] = jnp.where(first, low, high)
    ref.r_pair[:, COLS : 2 * COLS] = jnp.where(first, high, low)
    targets = (ref.r_wo, ref.r_q, ref.r_k, ref.r_v)
    for k, first_part in ((blocks, 0), (blocks + 2, 2), (blocks + 3, 4)):
        for part in range(2):
            for source, off, width, at in late_pieces(half, first_part + part):
                targets[source][:, off : off + width] = fin[k, part, 0:sh, at : at + width]
    for save in saves:
        save.wait()
    save_b.wait()


def unpack(T, D, FH, sh, sp, out):
    half = D // 2
    blocks = FH // COLS
    count = 4
    inputs = dict(o_blk=out.o_blk, o_tok=out.o_tok, o_norm=out.o_norm, o_fin=out.o_fin)
    vector, square, wide = (VMEM, (half,), f32), (VMEM, (sh, half), f32), (VMEM, (sh, FH), f32)
    results = dict(
        r_blk=(ANY, (2 * T, half), bf16), r_tok=(ANY, (2 * T, half), f32), r_gi=vector, r_si=vector, r_q=square,
        r_k=square, r_v=square, r_wo=square, r_gm=vector, r_sm=vector, r_up=wide, r_dn=wide,
        r_pair=(VMEM, (sp, T // 2), f32),
    )
    scratch = dict(
        blk=pltpu.VMEM((2 * T, half), bf16), tok_in=pltpu.VMEM((2 * T, half), bf16),
        tok_out=pltpu.VMEM((2 * T, half), f32), sem=pltpu.SemaphoreType.DMA((2, 2 + count)),
        fin=pltpu.VMEM(out.o_fin.shape, f32), norm=pltpu.VMEM((8, half), f32),
    )
    values = pl.pallas_call(
        functools.partial(unpack_kernel, sh, blocks, half, count, tuple(inputs) + tuple(results) + tuple(scratch)),
        out_shape=tuple(jax.ShapeDtypeStruct(shape, kind) for _, shape, kind in results.values()),
        in_specs=[ANY] * len(inputs),
        out_specs=tuple(spec for spec, _, _ in results.values()),
        scratch_shapes=list(scratch.values()),
        compiler_params=pltpu.CompilerParams(vmem_limit_bytes=63 << 20),
    )(*inputs.values())
    blk, tok, gi, si, q, k, v, wo, gm, sm, up, dn, pair = values
    return blk, tok, gi, si, q, k, v, wo.T, gm, sm, up, dn.T, pair


def gather_parts(T, D, R, nb, sp, out, pair_bias):
    half = D // 2
    parts = out.GO
    blocks = parts.shape[0] - 4
    height = lambda v, rows: v.reshape(nb, sp, v.shape[-1])[:, : rows // nb].reshape(rows, v.shape[-1])
    join = lambda chosen: jnp.concatenate(chosen, 1).astype(f32)
    scatter = lambda v: lax.psum_scatter(v, "rows", scatter_dimension=0, tiled=True)
    up = scatter(join([height(parts[k, 0], D) for k in range(blocks)]))
    down = scatter(join([height(parts[k, 1], D) for k in range(blocks)])).T
    late = join([height(parts[k, p], D) for k in (blocks, blocks + 2, blocks + 3) for p in range(2)])
    wo, q, k, v = (scatter(late[:, i * half : (i + 1) * half]) for i in range(4))
    first = lax.axis_index("chan") == 0
    low, high = (height(parts[blocks + 1, p], T) for p in range(2))
    pair = scatter(join([jnp.where(first, low, high), jnp.where(first, high, low)]))
    bias = lax.dynamic_slice(
        pair_bias, (lax.axis_index("rows") * pair.shape[0], lax.axis_index("chan") * (T // 2)), pair.shape
    )
    norms = lax.psum(out.o_norm, "rows")
    return (
        out.o_blk, out.o_tok.astype(f32), norms[0], norms[1], q, k, v, wo.T, norms[2], norms[3], up, down,
        pair * jnp.exp(bias),
    )


def on_device(
    tokens, segments, gain_in, shift_in, query_weight, key_weight, value_weight, out_weight,
    gain_mid, shift_mid, up_weight, down_weight, pair_bias, out_grad,
):
    T = segments.shape[1]
    D, FH = up_weight.shape
    R = lax.axis_size("rows")
    half = D // 2
    blocks = FH // COLS
    fused = R == 16 and D % (16 * R) == 0 and T % (16 * R) == 0
    nb = R if fused else 16
    nz = nb // 4
    sh, sp = D // nb, T // nb
    inputs = dict(
        tokens=tokens, segments=segments, gi=gain_in, si=shift_in, wq=query_weight, wk=key_weight, wv=value_weight,
        wo=out_weight, gm=gain_mid, sm=shift_mid, wu=up_weight, wd=down_weight, pair_bias=pair_bias,
        out_grad=out_grad,
    )
    near = ("segments", "gi", "si", "gm", "sm")
    outputs = dict(
        o_blk=(ANY, (2 * T, half), bf16), o_tok=(ANY, (2 * T, half), bf16), o_norm=(VMEM, (8, half), f32)
    )
    if fused:
        outputs |= dict(o_fin=(ANY, (blocks + 4, 2, sp, COLS), f32))
    else:
        outputs |= dict(GO=(ANY, (blocks + 4, 2, nb, sp, COLS), bf16))
    square, act, total = pltpu.VMEM((D, D), bf16), pltpu.VMEM((T, D), bf16), pltpu.VMEM((T, D), f32)
    small, halves = pltpu.VMEM((8, TILE), f32), pltpu.VMEM((8, half), f32)
    sems = pltpu.SemaphoreType.DMA
    scratch = dict(
        XB=act, OG=act, HN=act, G=act, Y=act, QQ=act, RT=act, RZ=act, T2=act,
        AB=pltpu.VMEM((T, 2 * D), bf16), MM=pltpu.VMEM((T, T), bf16), F1=total, F3=total,
        ST=pltpu.VMEM((T, TILE), f32), WQ=square, WK=square, WV=square, WO=square,
        WU=pltpu.VMEM((2 * D, FH), bf16), WD=pltpu.VMEM((2 * FH, D), bf16),
        SD=pltpu.VMEM((T, 2 * COLS), bf16), SC=pltpu.VMEM((T, TILE), f32),
        NP=pltpu.VMEM((8, D), f32), NPS=halves, NPR=halves,
        PS=pltpu.VMEM((2, 2, T, COLS), bf16), PR=pltpu.VMEM((2, 2, T, COLS), bf16),
        S=pltpu.VMEM((SLOTS, 2, nb, sp, COLS), bf16),
        RX=pltpu.VMEM((SLOTS, 2, nb - 1, sp, COLS), bf16) if fused else small,
        FIN=pltpu.VMEM((blocks + 4, 2, sp, COLS), f32) if fused else small,
        NG=pltpu.VMEM((4, 8, D), f32), NV=pltpu.VMEM((8, D), f32), NR=pltpu.VMEM((5, 8, half), f32),
        NZS=pltpu.VMEM((nz, 8, half), f32), PBO=pltpu.VMEM((sp, T // 2), f32),
        local_sem=sems((16,)), entry_s=sems((16,)), entry_r=sems((16,)), end_l=sems((2,)), end_s=sems((2,)),
        end_r=sems((2,)), up_l=sems((blocks // 2,)), up_s=sems((blocks // 2,)), up_r=sems((blocks // 2,)),
        down_l=sems((blocks // 2,)), down_s=sems((blocks // 2,)), down_r=sems((blocks // 2,)),
        pair_s=sems((2, 5)), pair_r=sems((2, 5)), ring_s=sems((SLOTS, 2, 6)), ring_r=sems((SLOTS, 2, 6)),
        norm_s=sems((2 + nz,)), norm_r=sems((2 + nz,)), fin_sem=sems((blocks + 4, 2)),
    )
    results = pl.pallas_call(
        functools.partial(
            block_kernel, T, D, FH, R, fused, tuple(inputs) + tuple(outputs) + tuple(scratch)
        ),
        out_shape=tuple(jax.ShapeDtypeStruct(shape, kind) for _, shape, kind in outputs.values()),
        in_specs=[VMEM if name in near else ANY for name in inputs],
        out_specs=tuple(spec for spec, _, _ in outputs.values()),
        scratch_shapes=list(scratch.values()),
        compiler_params=pltpu.CompilerParams(
            collective_id=0, has_side_effects=True, vmem_limit_bytes=63 << 20
        ),
    )(*inputs.values())
    out = SimpleNamespace(**dict(zip(outputs, results)))
    if fused:
        return unpack(T, D, FH, sh, sp, out)
    return gather_parts(T, D, R, nb, sp, out, pair_bias)


def solution(mesh):
    split, first, second, vector = P("rows", "chan"), P("chan", None), P(None, "chan"), P("chan")
    return jax.shard_map(
        on_device,
        mesh=mesh,
        in_specs=(
            split, P("rows", None), vector, vector, second, second, second, first, vector, vector, second, first,
            P(), split,
        ),
        out_specs=(
            split, split, vector, vector, split, split, split, P("chan", "rows"), vector, vector, split,
            P("chan", "rows"), split,
        ),
        check_vma=False,
    )
```

time: 128 us -> 115 us (0.90)
  Pallas kernels: 127 us -> 114 us
    pallas_call x2, Pallas kernels: 127 us -> 114 us  [the longest x1 110 us: on_device(): pl.pallas_call(functools.partial(block_kernel, T, D, FH, R, fused, tuple(...]
where the time goes in v3:
time: 115 us
  Pallas kernels  114 us (99%)
    pallas_call x1, Pallas kernels, on_device(): pl.pallas_call(functools.partial(block_kernel, T, D, FH, R, fused, tuple(...  110 us
    pallas_call x1, Pallas kernels, unpack(): pl.pallas_call(functools.partial(unpack_kernel, sh, blocks, half, count,...  4.53 us

profile of v3, /device:TPU:0, one launch (start us, length us, event | category | flops | bytes accessed | tf_op | source)
XLA Modules:
  0.0 115.2 jit_solution(4809330352309508438)
XLA Ops:
  0.7 109.9 %shard_map.237 = (bf16[2048,384]{1,0:T(8,128)(2,1)}, bf16[2048,384]{1,0:T(8,128)(2,1)}, f32[8,384]{1,0:T(8,128)}, f32[10,2,64,256]{3,2,1,0:T(8,128)}) custom-call(bf16[2048,384]{1,0:T(8,128)(2,1)} %all_refs_0_.1, s32[2,1024]{1,0:T(2,128)} %all_refs_1_.1, f32[384]{0:T(512)} %all_refs_2_.1, f32[384]{0:T(512)} %all_refs_3_.1, bf16[768,384]{1,0:T(8,128)(2,1)} %all_refs_4_.1, ...), custom_call_target="tpu_custom_call" | custom-call | tf_op jit(solution)/shard_map/pallas_call | solution.py:739
  110.5 4.5 %shard_map.238 = (bf16[2048,384]{1,0:T(8,128)(2,1)}, f32[2048,384]{1,0:T(8,128)}, f32[384]{0:T(512)}, f32[384]{0:T(512)}, f32[48,384]{1,0:T(8,128)}, /*index=5*/...) custom-call(bf16[2048,384]{1,0:T(8,128)(2,1)} %get-tuple-element.30., ...), custom_call_target="tpu_custom_call" | custom-call | tf_op jit(solution)/shard_map/pallas_call | solution.py:655

commit v4 on v3

v4 whole, which is shorter than its diff:
```python
import functools
from types import SimpleNamespace

import jax
import jax.numpy as jnp
from jax import lax
from jax.experimental import pallas as pl
from jax.experimental.pallas import tpu as pltpu
from jax.sharding import PartitionSpec as P

MESH = pl.DeviceIdType.MESH
ANY, VMEM = pl.BlockSpec(memory_space=pl.ANY), pl.BlockSpec(memory_space=pltpu.VMEM)
WIN = 256
EPSILON = 1e-05
TILE = 128
COLS = 256
SLOTS = 6
STEP = 256
LAGS = (2, 3, 4)
LATE = (
    ((-3, 2), (-2, 1)), (), ((-4, 3), (-2, 2), (-1, 1)), (), ((0, 1),), ((-1, 2),), ((-3, 3), (-2, 3)), ((0, 2), (1, 1)),
    ((2, 1),), ((1, 2),), ((0, 3), (2, 2)), ((3, 1),), ((-1, 3), (4, 1)), ((3, 2),), ((1, 3), (4, 2)),
    ((2, 3), (3, 3), (4, 3)),
)
f32 = jnp.float32
bf16 = jnp.bfloat16


def dot(left, right, cl=1, cr=0):
    return lax.dot_general(left, right, (((cl,), (cr,)), ((), ())), preferred_element_type=f32)


def dot_nt(left, right):
    return dot(left, right, 1, 1)


def dot_tn(left, right):
    return dot(left, right, 0, 0)


def gelu_pair(p):
    phi = 0.5 * (1.0 + lax.erf(p * 0.7071067811865476))
    return p * phi, phi + p * (jnp.exp(-0.5 * p * p) * 0.3989422804014327)


def fold_rows(v):
    return jnp.sum(v.reshape(v.shape[0] // 8, 8, v.shape[1]), axis=0)


def widths_of(half, late):
    return (COLS, half - COLS) if late % 2 == 0 else (half - COLS, COLS)


def block_kernel(T, D, FH, R, fused, names, *all_refs):
    ref = SimpleNamespace(**dict(zip(names, all_refs)))
    half = D // 2
    blocks = FH // COLS
    nb = R if fused else 16
    nz = nb // 4
    sh, sp = D // nb, T // nb
    r = lax.axis_index("rows")
    c = lax.axis_index("chan")
    o = 1 - c
    mx, my, mz = lax.rem(r, 2), lax.rem(r // 2, 2), r // 4
    z0, z1 = lax.rem(mz, 2), mz // 2
    dev_c = (r, o)
    dev_x = (r + 1 - 2 * mx, c)
    dev_y = (r + 2 - 4 * my, c)
    z0, z1 = lax.rem(mz, 2), mz // 2
    dev_z = [(lax.rem(mz + j, nz) * 4 + lax.rem(r, 4), c) for j in range(1, nz)]
    dev_z0, dev_z1 = (r + 4 - 8 * z0, c), (r + 8 - 16 * z1, c)
    dev_z0 = (r + 4 - 8 * z0, c)
    dev_z1 = (r + 8 - 16 * z1, c)
    own_half = pl.ds(pl.multiple_of(c * half, TILE), half)
    other_half = pl.ds(pl.multiple_of(o * half, TILE), half)

    XB, OG, HN, G = ref.XB, ref.OG, ref.HN, ref.G
    Y, QQ, RT, RZ, T2 = ref.Y, ref.QQ, ref.RT, ref.RZ, ref.T2
    AB, MM, F1, F3, ST = ref.AB, ref.MM, ref.F1, ref.F3, ref.ST
    WQ, WK, WV, WO, WU, WD = ref.WQ, ref.WK, ref.WV, ref.WO, ref.WU, ref.WD
    SD, SC, NP, NPS, NPR = ref.SD, ref.SC, ref.NP, ref.NPS, ref.NPR
    PS, PR, S, RX, FIN = ref.PS, ref.PR, ref.S, ref.RX, ref.FIN
    NG, NV, NR, NZS = ref.NG, ref.NV, ref.NR, ref.NZS

    def remote(src, dst, send, recv, device):
        return pltpu.make_async_remote_copy(
            src_ref=src, dst_ref=dst, send_sem=send, recv_sem=recv, device_id=device, device_id_type=MESH
        )

    my_rows, other_rows = pl.ds(c * T, T), pl.ds(o * T, T)
    h2 = T // 2
    local, cross = [], []

    def load(src, dst, away=None, there=None):
        at = len(local)
        local.append(pltpu.make_async_copy(src, dst, ref.local_sem.at[at]))
        cross.append(None if away is None else remote(away, there, ref.entry_s.at[at], ref.entry_r.at[at], dev_c))
        local[at].start()
        return at

    bias_at = [
        load(ref.pair_bias.at[0:h2, 0:D], F3.at[0:h2, :]),
        load(ref.pair_bias.at[h2:T, T - D : T], F3.at[h2:T, :]),
    ]
    tokens_at = load(
        ref.tokens.at[my_rows, :], XB.at[:, own_half], ref.tokens.at[other_rows, :], XB.at[:, own_half]
    )
    qkv_at = [
        load(src, dst.at[:, 0:half], src, dst.at[:, half:D]) for src, dst in ((ref.wk, WK), (ref.wv, WV), (ref.wq, WQ))
    ]
    wo_at = load(ref.wo, WO.at[0:half, :], ref.wo, WO.at[half:D, :])
    og_at = load(
        ref.out_grad.at[my_rows, :], OG.at[:, own_half], ref.out_grad.at[other_rows, :], OG.at[:, own_half]
    )
    wide, per_row = 2 * COLS, blocks // 2

    def up_block(i, at=0, width=wide):
        rows = pl.ds(pl.multiple_of(i // per_row * D, TILE), D)
        return rows, pl.ds(pl.multiple_of(lax.rem(i, per_row) * wide + at, COLS), width)

    def down_block(i, at=0, width=wide):
        return pl.ds(pl.multiple_of(i * wide + at, COLS), width)

    def hidden_copies(i):
        part = pl.ds(pl.multiple_of(i * COLS, COLS), COLS)
        up, down = ref.wu.at[:, part], ref.wd.at[part, :]
        return (
            pltpu.make_async_copy(up, WU.at[up_block(i, 0, COLS)], ref.up_l.at[i]),
            pltpu.make_async_copy(down, WD.at[down_block(i, 0, COLS), :], ref.down_l.at[i]),
            remote(up, WU.at[up_block(i, COLS, COLS)], ref.up_s.at[i], ref.up_r.at[i], dev_c),
            remote(down, WD.at[down_block(i, COLS, COLS), :], ref.down_s.at[i], ref.down_r.at[i], dev_c),
        )

    pbo_at = None
    if fused:
        pair_rows = pl.ds(pl.multiple_of(r * sp, 8), sp)
        pair_cols = pl.ds(pl.multiple_of(c * (T // 2), TILE), T // 2)
        pbo_at = load(ref.pair_bias.at[pair_rows, pair_cols], ref.PBO)
    hidden_weights = [hidden_copies(jnp.int32(i)) for i in range(blocks)]
    for copies in hidden_weights:
        copies[0].start()
        copies[1].start()

    NPS[...] = jnp.zeros(NPS.shape, f32)
    for i, vector in enumerate((ref.gi, ref.si, ref.gm, ref.sm)):
        NPS[i : i + 1, :] = vector[...].reshape(1, half)
    norms_cross = remote(NPS, NPR, ref.entry_s.at[15], ref.entry_r.at[15], dev_c)
    barrier = pltpu.get_barrier_semaphore()
    greeted = [dev_c] + ([dev_x, dev_y] + dev_z if fused else [])
    for device in greeted:
        pl.semaphore_signal(barrier, inc=1, device_id=device, device_id_type=MESH)
    pl.semaphore_wait(barrier, len(greeted))
    norms_cross.start()
    for at in [tokens_at] + qkv_at:
        cross[at].start()

    def ready(*chosen):
        for at in chosen:
            local[at].wait()
            if cross[at] is not None:
                cross[at].wait()

    seg = ref.segments[pl.ds(c, 1), :].astype(f32)
    SC[...] = jnp.broadcast_to(seg, (TILE, T)).T.astype(bf16)
    ready(*bias_at)
    row_id = lax.broadcasted_iota(jnp.int32, (TILE, TILE), 0)
    col_id = lax.broadcasted_iota(jnp.int32, (TILE, TILE), 1)
    for a in range(T // TILE):
        rows = slice(a * TILE, (a + 1) * TILE)
        shift = 0 if a * TILE < h2 else T - D
        for b in range(T // TILE):
            cols = slice(b * TILE, (b + 1) * TILE)
            far = abs(a - b) * TILE
            if far - TILE + 1 >= T // 2:
                MM[rows, cols] = jnp.zeros((TILE, TILE), bf16)
                continue
            same = SC[rows, :].astype(f32) == seg[:, cols]
            if far - TILE + 1 >= WIN:
                weight = jnp.ones((TILE, TILE), f32)
            else:
                weight = jnp.exp(F3[rows, b * TILE - shift : (b + 1) * TILE - shift])
                if far + TILE - 1 >= WIN:
                    inside = jnp.abs(row_id - col_id + (a - b) * TILE) < WIN
                    weight = jnp.where(inside, weight, 1.0)
            MM[rows, cols] = jnp.where(same, weight, 0.0).astype(bf16)

    norms_cross.wait()
    for i in range(4):
        NP[i : i + 1, own_half] = NPS[i : i + 1, :]
        NP[i : i + 1, other_half] = NPR[i : i + 1, :]
    ready(tokens_at)

    def norm_in(i, carry):
        rows = pl.ds(i * STEP, STEP)
        x = XB[rows, :].astype(f32)
        centred = x - jnp.mean(x, axis=1, keepdims=True)
        inv = lax.rsqrt(jnp.mean(centred * centred, axis=1, keepdims=True) + EPSILON)
        t = centred * inv
        F1[rows, :] = x
        XB[rows, :] = t.astype(bf16)
        HN[rows, :] = (t * NP[0:1, :] + NP[1:2, :]).astype(bf16)
        ST[rows, 0:1] = inv
        return carry

    lax.fori_loop(0, T // STEP, norm_in, 0)
    cross[wo_at].start()
    cross[og_at].start()
    for copies in hidden_weights:
        copies[2].start()
        copies[3].start()
    for at in qkv_at:
        local[at].wait()

    for j in range(D // COLS):
        if j * COLS <= half < (j + 1) * COLS:
            for at in qkv_at:
                cross[at].wait()
        cols = slice(j * COLS, (j + 1) * COLS)
        late = slice(D + j * COLS, D + (j + 1) * COLS)
        e = jnp.exp(dot(HN[...], WK[:, cols]))
        a = (e * dot(HN[...], WV[:, cols])).astype(bf16)
        AB[:, cols] = a
        AB[:, late] = e.astype(bf16)
        gate = jax.nn.sigmoid(dot(HN[...], WQ[:, cols]))
        inv = 1.0 / dot(MM[...], AB[:, late])
        ratio = dot(MM[...], AB[:, cols]) * inv
        y = gate * ratio
        Y[:, cols] = y.astype(bf16)
        QQ[:, cols] = (y * (1.0 - gate)).astype(bf16)
        RT[:, cols] = ratio.astype(bf16)
        RZ[:, cols] = (gate * inv).astype(bf16)

    ready(wo_at)
    for i in range(T // STEP):
        rows = slice(i * STEP, (i + 1) * STEP)
        x = F1[rows, :] + dot(Y[rows, :], WO[...])
        F1[rows, :] = x
        centred = x - jnp.mean(x, axis=1, keepdims=True)
        inv = lax.rsqrt(jnp.mean(centred * centred, axis=1, keepdims=True) + EPSILON)
        t = centred * inv
        T2[rows, :] = t.astype(bf16)
        G[rows, :] = (t * NP[2:3, :] + NP[3:4, :]).astype(bf16)
        ST[rows, 1:2] = inv
        F3[rows, :] = jnp.zeros((STEP, D), f32)
    ready(og_at)
    if fused:
        ready(pbo_at)

    ex, ey, ez0, ez1 = (mx, dev_x), (my, dev_y), (z0, dev_z0), (z1, dev_z1)
    halvings = (((ex, ey), (ey, ex)), ((ex, ez0, ez1, ey), (ey, ez0, ez1, ex)))

    def chunk(k, wind=(0, 0), widths=(COLS, COLS)):
        return SimpleNamespace(
            k=k, slot=lax.rem(k, SLOTS), wind=wind, widths=widths, height=sh, counts=(nz, nz),
            index=(lambda z: z, lambda z: z), valid=(None, None), late=False,
        )

    def late_chunk(late):
        widths = (COLS, COLS) if late == 2 else widths_of(half, late if late < 2 else late - 1)
        ch = chunk(jnp.int32(blocks + late), widths=widths)
        ch.late = True
        if late == 2:
            ch.height = sp
        if late == 2 and fused:
            ch.counts = (2, 3)
            ch.index = (lambda z: lax.rem(z, 2), lambda z: lax.rem(z + 3 - c, 3))
            ch.valid = (mz // 2 == c, mz != 3 * o)
        return ch

    def place(ch, b, part):
        if not fused:
            return b
        bx, by, bz = b % 2, (b // 2) % 2, b // 4
        outer, inner = (bx, by) if part == 0 else (by, bx)
        if ch.wind[part]:
            return ((outer * 2 + bz % 2) * 2 + bz // 2) * 2 + inner
        return (outer * 2 + inner) * ch.counts[part] + bz

    def form(ch, part, own, total_rows):
        width, height = ch.widths[part], ch.height
        for b in range(total_rows // height):
            rows = slice(b * height, (b + 1) * height)
            at = place(ch, b, part) * height
            S[ch.slot, part, at : at + height, 0:width] = (
                own[rows, :].astype(bf16) + PR[lax.rem(ch.k, 2), part, rows, 0:width]
            )

    def block_rows(ch, first, count):
        return pl.ds(pl.multiple_of(first * ch.height, 16), count * ch.height)

    def stages(ch, part):
        return 4 if ch.wind[part] else 3

    def span(ch, part, n):
        base, size = 0, nb if ch.wind[part] else 4 * ch.counts[part]
        for bit, _ in halvings[ch.wind[part]][part][: n - 1]:
            size //= 2
            base = base + bit * size
        return base, size

    def landing(ch, part, n):
        if ch.wind[part]:
            return (0, nb // 2, 3 * nb // 4, nb - 2)[n - 1]
        return (0, 2, 3)[n - 1] * ch.counts[part]

    def stage(ch, part, n):
        cols, copies = pl.ds(0, ch.widths[part]), []
        base, size = span(ch, part, n)
        plan = halvings[ch.wind[part]][part]
        if n <= len(plan):
            bit, device = plan[n - 1]
            moves = [(base + (1 - bit) * (size // 2), landing(ch, part, n), size // 2, device)]
        else:
            moves = [
                (base + ch.index[part](lax.rem(mz + j, nz)), landing(ch, part, n) + j - 1, 1, dev_z[j - 1])
                for j in range(1, nz)
            ]
        for i, (first, at, count, device) in enumerate(moves):
            copies.append(remote(
                S.at[ch.slot, part, block_rows(ch, first, count), cols],
                RX.at[ch.slot, part, block_rows(ch, at, count), cols],
                ref.ring_s.at[ch.slot, part, n - 1 + i], ref.ring_r.at[ch.slot, part, n - 1 + i], device,
            ))
        return copies

    def whole(ch):
        return pltpu.make_async_copy(S.at[ch.slot], ref.GO.at[ch.k], ref.ring_s.at[ch.slot, 0, 0])

    def fin_copy(ch, part):
        rows, cols = pl.ds(0, ch.height), pl.ds(0, ch.widths[part])
        return pltpu.make_async_copy(
            FIN.at[lax.rem(ch.k, SLOTS), part, rows, cols], ref.o_fin.at[ch.k, part, rows, cols], ref.fin_sem.at[ch.k, part]
        )

    def launch(ch):
        if not fused:
            whole(ch).start()
            return
        for part in range(2):
            for copy in stage(ch, part, 1):
                copy.start()

    def advance(ch, n):
        if not fused:
            if n == 1:
                whole(ch).wait()
            return
        for part in range(2):
            last = stages(ch, part)
            if n > last:
                continue
            for copy in stage(ch, part, n):
                copy.wait()
            cols, at = slice(0, ch.widths[part]), landing(ch, part, n)
            base, size = span(ch, part, n + 1)
            if n < last:
                S[ch.slot, part, block_rows(ch, base, size), cols] += RX[ch.slot, part, block_rows(ch, at, size), cols]
                for copy in stage(ch, part, n + 1):
                    copy.start()
                continue
            mine = base if ch.wind[part] else base + ch.index[part](mz)
            total = S[ch.slot, part, block_rows(ch, mine, 1), cols].astype(f32)
            for j in range(1 if ch.wind[part] else nz - 1):
                total = total + RX[ch.slot, part, block_rows(ch, at + j, 1), cols].astype(f32)
            if ch.valid[part] is not None:
                bias = ref.PBO[:, pl.ds(pl.multiple_of(pair_part[part] * COLS, COLS), COLS)]
                total = jnp.where(ch.valid[part], total * jnp.exp(bias), 0.0)
            if ch.late:
                fin_copy(chunk(ch.k - SLOTS), part).wait()
            FIN[lax.rem(ch.k, SLOTS), part, 0 : ch.height, cols] = total
            fin_copy(ch, part).start()

    def pair_copy(slot):
        return remote(PS.at[slot], PR.at[slot], ref.pair_s.at[slot, 0], ref.pair_r.at[slot, 0], dev_c)

    def hidden_round(i, carry):
        for copy in hidden_copies(i):
            copy.wait()
        up_at, down_at = up_block(i), down_block(i)
        s, slope = gelu_pair(dot(G[...], WU[up_at]))
        SD[:, 0:wide] = s.astype(bf16)
        SD[:, wide:] = (dot_nt(OG[...], WD[down_at, :]) * slope).astype(bf16)
        for n, lag in enumerate(LAGS):
            pl.when(i >= lag)(functools.partial(advance, chunk(i - lag), n + 1))
        slot = lax.rem(i, 2)
        PS[slot, 0] = dot_tn(G[...], SD[:, wide + COLS :]).astype(bf16)
        PS[slot, 1] = dot_tn(OG[...], SD[:, COLS:wide]).astype(bf16)
        pair_copy(slot).start()
        F1[...] += dot(SD[:, 0:wide], WD[down_at, :])
        F3[...] += dot_nt(SD[:, wide:], WU[up_at])
        up = dot_tn(G[...], SD[:, wide : wide + COLS])
        down = dot_tn(OG[...], SD[:, 0:COLS])
        pair_copy(slot).wait()
        ch = chunk(i)
        form(ch, 0, up, D)
        form(ch, 1, down, D)
        launch(ch)
        return carry

    lax.fori_loop(0, blocks, hidden_round, 0)
    pair_part = (c, 1 - c)

    def pump(*steps):
        for late, n in steps:
            if late >= 0:
                advance(late_chunk(late), n)
            else:
                advance(chunk(jnp.int32(blocks + late)), n)

    NG[...] = jnp.zeros(NG.shape, f32)

    def norm_mid_back(i, carry):
        rows = pl.ds(i * STEP, STEP)
        G[rows, :] = F1[rows, :].astype(bf16)
        grad, t = F3[rows, :], T2[rows, :].astype(f32)
        w = grad * NP[2:3, :]
        mean_w = jnp.mean(w, axis=1, keepdims=True)
        mean_wt = jnp.mean(w * t, axis=1, keepdims=True)
        dx = OG[rows, :].astype(f32) + ST[rows, 1:2] * (w - mean_w - t * mean_wt)
        F3[rows, :] = dx
        T2[rows, :] = dx.astype(bf16)
        NG[2] += fold_rows(grad * t)
        NG[3] += fold_rows(grad)
        return carry

    lax.fori_loop(0, T // STEP, norm_mid_back, 0)
    blk_local = pltpu.make_async_copy(G.at[:, own_half], ref.o_blk.at[my_rows, :], ref.end_l.at[0])
    blk_cross = remote(G.at[:, other_half], ref.o_blk.at[my_rows, :], ref.end_s.at[0], ref.end_r.at[0], dev_c)
    blk_local.start()
    blk_cross.start()
    pump(*LATE[0])

    half_cols = (slice(0, half), slice(half, D))

    def late_copies(late, source):
        ch, copies, at = late_chunk(late), [], half
        for part, width in enumerate(ch.widths):
            copies.append(remote(
                source.at[pl.ds(0, D), pl.ds(at, width)], PR.at[late % 2, part, :, pl.ds(0, width)],
                ref.pair_s.at[late % 2, 1 + part], ref.pair_r.at[late % 2, 1 + part], dev_c,
            ))
            at += width
        for copy in copies:
            copy.start()
        return copies

    def late_form(late, source, copies):
        for copy in copies:
            copy.wait()
        ch, at = late_chunk(late), 0
        for part, width in enumerate(ch.widths):
            form(ch, part, source.at[pl.ds(0, D), pl.ds(at, width)], D)
            at += width
        launch(ch)

    NZ = WU

    def gate_back(j):
        cols = slice(j * COLS, (j + 1) * COLS)
        late = slice(D + j * COLS, D + (j + 1) * COLS)
        dm = dot_nt(T2[...], WO[cols, :])
        QQ[:, cols] = (dm * QQ[:, cols].astype(f32)).astype(bf16)
        dn = dm * RZ[:, cols].astype(f32)
        NZ[0:T, cols] = dn.astype(bf16)
        NZ[0:T, late] = (-dn * RT[:, cols].astype(f32)).astype(bf16)

    OG[0:D, :] = dot_tn(T2[...], Y[...]).astype(bf16)
    sent = late_copies(0, OG)
    gate_back(0)
    gate_back(1)
    pump(*LATE[1])
    late_form(0, OG, sent)
    gate_back(2)
    RZ[0:D, :] = dot_tn(HN[...], QQ[...]).astype(bf16)
    sent = late_copies(1, RZ)
    pump(*LATE[2])

    def mixer_grad(j):
        cols = slice(j * COLS, (j + 1) * COLS)
        low, high = max(0, (j - 1) * COLS), min(T, (j + 2) * COLS)
        target = PS.at[j // 2, j if j < 2 else 3 - j]
        grad = dot_nt(NZ[low:high, :], AB[cols, :])
        for t in range(COLS // TILE):
            at = j * COLS + t * TILE
            same = SC[low:high, :].astype(f32) == seg[:, at : at + TILE]
            gap = (
                lax.broadcasted_iota(jnp.int32, (high - low, TILE), 0)
                - lax.broadcasted_iota(jnp.int32, (high - low, TILE), 1)
                + (low - at)
            )
            kept = jnp.where(same & (jnp.abs(gap) < WIN), grad[:, t * TILE : (t + 1) * TILE], 0.0)
            target[0 : high - low, t * TILE : (t + 1) * TILE] = kept.astype(bf16)

    mixer_rows = (2 * COLS, 3 * COLS)
    mixer_grad(0)
    mixer_grad(1)
    pump(*LATE[3])
    late_form(1, RZ, sent)
    mixer_grad(2)
    mixer_grad(3)
    mixer_copies = [
        remote(
            PS.at[o, part, pl.ds(0, mixer_rows[part]), :], PR.at[0, part, pl.ds(0, mixer_rows[part]), :],
            ref.pair_s.at[0, 3 + part], ref.pair_r.at[0, 3 + part], dev_c,
        )
        for part in range(2)
    ]
    for copy in mixer_copies:
        copy.start()
    pump(*LATE[4])

    def mixing_back(j):
        cols = slice(j * COLS, (j + 1) * COLS)
        late = slice(D + j * COLS, D + (j + 1) * COLS)
        da = dot_tn(MM[...], NZ[0:T, cols])
        db = dot_tn(MM[...], NZ[0:T, late])
        e = AB[:, late].astype(f32)
        T2[:, cols] = (db * e + da * AB[:, cols].astype(f32)).astype(bf16)
        Y[:, cols] = (da * e).astype(bf16)

    mixing_back(0)
    pump(*LATE[5])
    for copy in mixer_copies:
        copy.wait()
    for part in range(2):
        form(late_chunk(2), part, PS.at[c, part], mixer_rows[part])
    launch(late_chunk(2))
    mixing_back(1)
    mixing_back(2)
    pump(*LATE[6])
    RT[0:D, :] = dot_tn(HN[...], T2[...]).astype(bf16)
    sent = late_copies(3, RT)
    pump(*LATE[7])
    AB[0:D, 0:D] = dot_tn(HN[...], Y[...]).astype(bf16)
    pump(*LATE[8])
    late_form(3, RT, sent)
    sent = late_copies(4, AB)

    def norm_in_grad(j):
        cols = slice(j * COLS, (j + 1) * COLS)
        F1[:, cols] = dot_nt(QQ[...], WQ[cols, :]) + dot_nt(T2[...], WK[cols, :]) + dot_nt(Y[...], WV[cols, :])

    norm_in_grad(0)
    pump(*LATE[9])
    late_form(4, AB, sent)
    norm_in_grad(1)
    pump(*LATE[10])
    norm_in_grad(2)
    pump(*LATE[11])

    def norm_in_back(i, carry):
        rows = pl.ds(i * STEP, STEP)
        grad, t = F1[rows, :], XB[rows, :].astype(f32)
        w = grad * NP[0:1, :]
        mean_w = jnp.mean(w, axis=1, keepdims=True)
        mean_wt = jnp.mean(w * t, axis=1, keepdims=True)
        HN[rows, :] = (F3[rows, :] + ST[rows, 0:1] * (w - mean_w - t * mean_wt)).astype(bf16)
        NG[0] += fold_rows(grad * t)
        NG[1] += fold_rows(grad)
        return carry

    lax.fori_loop(0, T // STEP, norm_in_back, 0)
    tok_local = pltpu.make_async_copy(HN.at[:, own_half], ref.o_tok.at[my_rows, :], ref.end_l.at[1])
    tok_cross = remote(HN.at[:, other_half], ref.o_tok.at[my_rows, :], ref.end_s.at[1], ref.end_r.at[1], dev_c)
    tok_local.start()
    tok_cross.start()

    NV[...] = jnp.zeros(NV.shape, f32)
    for i in range(4):
        NV[i : i + 1, :] = jnp.sum(NG[i], axis=0, keepdims=True)
    copy = remote(NV.at[:, other_half], NR.at[0], ref.norm_s.at[0], ref.norm_r.at[0], dev_c)
    copy.start()
    pump(*LATE[12])
    copy.wait()
    NR[1] = NV[:, own_half] + NR[0]
    if fused:
        copy = remote(NR.at[1], NR.at[2], ref.norm_s.at[1], ref.norm_r.at[1], dev_x)
        copy.start()
        pump(*LATE[13])
        copy.wait()
        NR[3] = NR[1] + NR[2]
        copy = remote(NR.at[3], NR.at[4], ref.norm_s.at[2], ref.norm_r.at[2], dev_y)
        copy.start()
        pump(*LATE[14])
        copy.wait()
        NZS[mz] = NR[3] + NR[4]
        copies = [
            remote(NZS.at[mz], NZS.at[mz], ref.norm_s.at[2 + j], ref.norm_r.at[2 + j], dev_z[j - 1])
            for j in range(1, nz)
        ]
        for copy in copies:
            copy.start()
    pump(*LATE[15])
    if fused:
        for copy in copies:
            copy.wait()
        total = NZS[0]
        for j in range(1, nz):
            total = total + NZS[j]
        ref.o_norm[...] = total
        for k in range(blocks + 5 - SLOTS, blocks + 5):
            for part in range(2):
                fin_copy(late_chunk(k - blocks) if k >= blocks else chunk(jnp.int32(k)), part).wait()
    else:
        pump((4, 1))
        ref.o_norm[...] = NR[1]
    blk_local.wait()
    blk_cross.wait()
    tok_local.wait()
    tok_cross.wait()


def unpack_kernel(sh, blocks, half, count, names, *all_refs):
    ref = SimpleNamespace(**dict(zip(names, all_refs)))
    step = ref.tok_in.shape[0] // count
    load_b = pltpu.make_async_copy(ref.o_blk, ref.blk, ref.sem.at[0, 0])
    save_b = pltpu.make_async_copy(ref.blk, ref.r_blk, ref.sem.at[1, 0])
    loads, saves = [], []
    for i in range(count):
        rows = slice(i * step, (i + 1) * step)
        loads.append(pltpu.make_async_copy(ref.o_tok.at[rows, :], ref.tok_in.at[rows, :], ref.sem.at[0, 1 + i]))
        saves.append(pltpu.make_async_copy(ref.tok_out.at[rows, :], ref.r_tok.at[rows, :], ref.sem.at[1, 1 + i]))
    load_f = pltpu.make_async_copy(ref.o_fin, ref.fin, ref.sem.at[0, 1 + count])
    load_n = pltpu.make_async_copy(ref.o_norm, ref.norm, ref.sem.at[1, 1 + count])
    loads[0].start()
    load_b.start()
    for load in loads[1:]:
        load.start()
    load_f.start()
    load_n.start()
    fin, norm = ref.fin, ref.norm
    for i in range(count):
        loads[i].wait()
        rows = slice(i * step, (i + 1) * step)
        ref.tok_out[rows, :] = ref.tok_in[rows, :].astype(f32)
        saves[i].start()
        if i == 0:
            load_b.wait()
            save_b.start()
    load_n.wait()
    for i, vector in enumerate((ref.r_gi, ref.r_si, ref.r_gm, ref.r_sm)):
        vector[...] = norm[i, :]
    load_f.wait()
    for k in range(blocks):
        cols = slice(k * COLS, (k + 1) * COLS)
        ref.r_up[:, cols] = fin[k, 0, 0:sh, :]
        ref.r_dn[:, cols] = fin[k, 1, 0:sh, :]
    low, high = fin[blocks + 2, 0], fin[blocks + 2, 1]
    first = lax.axis_index("chan") == 0
    ref.r_pair[:, 0:COLS] = jnp.where(first, low, high)
    ref.r_pair[:, COLS : 2 * COLS] = jnp.where(first, high, low)
    for late, target in ((0, ref.r_wo), (1, ref.r_q), (3, ref.r_k), (4, ref.r_v)):
        at = 0
        for part, width in enumerate(widths_of(half, late if late < 2 else late - 1)):
            target[:, at : at + width] = fin[blocks + late, part, 0:sh, 0:width]
            at += width
    for save in saves:
        save.wait()
    save_b.wait()


def unpack(T, D, FH, sh, sp, out):
    half = D // 2
    blocks = FH // COLS
    count = 4
    inputs = dict(o_blk=out.o_blk, o_tok=out.o_tok, o_norm=out.o_norm, o_fin=out.o_fin)
    vector, square, wide = (VMEM, (half,), f32), (VMEM, (sh, half), f32), (VMEM, (sh, FH), f32)
    results = dict(
        r_blk=(ANY, (2 * T, half), bf16), r_tok=(ANY, (2 * T, half), f32), r_gi=vector, r_si=vector, r_q=square,
        r_k=square, r_v=square, r_wo=square, r_gm=vector, r_sm=vector, r_up=wide, r_dn=wide,
        r_pair=(VMEM, (sp, T // 2), f32),
    )
    scratch = dict(
        blk=pltpu.VMEM((2 * T, half), bf16), tok_in=pltpu.VMEM((2 * T, half), bf16),
        tok_out=pltpu.VMEM((2 * T, half), f32), sem=pltpu.SemaphoreType.DMA((2, 2 + count)),
        fin=pltpu.VMEM(out.o_fin.shape, f32), norm=pltpu.VMEM((8, half), f32),
    )
    values = pl.pallas_call(
        functools.partial(unpack_kernel, sh, blocks, half, count, tuple(inputs) + tuple(results) + tuple(scratch)),
        out_shape=tuple(jax.ShapeDtypeStruct(shape, kind) for _, shape, kind in results.values()),
        in_specs=[ANY] * len(inputs),
        out_specs=tuple(spec for spec, _, _ in results.values()),
        scratch_shapes=list(scratch.values()),
        compiler_params=pltpu.CompilerParams(vmem_limit_bytes=63 << 20),
    )(*inputs.values())
    blk, tok, gi, si, q, k, v, wo, gm, sm, up, dn, pair = values
    return blk, tok, gi, si, q, k, v, wo.T, gm, sm, up, dn.T, pair


def gather_parts(T, D, out, pair_bias):
    half = D // 2
    parts = out.GO
    blocks = parts.shape[0] - 5
    join = lambda chosen: jnp.concatenate(chosen, 1).astype(f32)
    scatter = lambda v: lax.psum_scatter(v, "rows", scatter_dimension=0, tiled=True)
    up = scatter(join([parts[k, 0] for k in range(blocks)]))
    down = scatter(join([parts[k, 1] for k in range(blocks)])).T
    late = []
    for i in (0, 1, 3, 4):
        widths = widths_of(half, i if i < 2 else i - 1)
        late.append(scatter(join([parts[blocks + i, p, :, 0:width] for p, width in enumerate(widths)])))
    wo, q, k, v = late
    first = lax.axis_index("chan") == 0
    spread = []
    for p, rows in ((0, 2 * COLS), (1, 3 * COLS)):
        held, rest = parts[blocks + 2, p, 0:rows], jnp.zeros((T - rows, COLS), bf16)
        spread.append(jnp.where(first, jnp.concatenate([held, rest]), jnp.concatenate([rest, held])))
    low, high = spread
    pair = scatter(join([jnp.where(first, low, high), jnp.where(first, high, low)]))
    bias = lax.dynamic_slice(
        pair_bias, (lax.axis_index("rows") * pair.shape[0], lax.axis_index("chan") * (T // 2)), pair.shape
    )
    norms = lax.psum(out.o_norm, "rows")
    return (
        out.o_blk, out.o_tok.astype(f32), norms[0], norms[1], q, k, v, wo.T, norms[2], norms[3], up, down,
        pair * jnp.exp(bias),
    )


def on_device(
    tokens, segments, gain_in, shift_in, query_weight, key_weight, value_weight, out_weight,
    gain_mid, shift_mid, up_weight, down_weight, pair_bias, out_grad,
):
    T = segments.shape[1]
    D, FH = up_weight.shape
    R = lax.axis_size("rows")
    half = D // 2
    blocks = FH // COLS
    fused = R == 16 and D % (16 * R) == 0 and T % (16 * R) == 0
    nb = R if fused else 16
    nz = nb // 4
    sh, sp = D // nb, T // nb
    inputs = dict(
        tokens=tokens, segments=segments, gi=gain_in, si=shift_in, wq=query_weight, wk=key_weight, wv=value_weight,
        wo=out_weight, gm=gain_mid, sm=shift_mid, wu=up_weight, wd=down_weight, pair_bias=pair_bias,
        out_grad=out_grad,
    )
    near = ("segments", "gi", "si", "gm", "sm")
    outputs = dict(
        o_blk=(ANY, (2 * T, half), bf16), o_tok=(ANY, (2 * T, half), bf16), o_norm=(VMEM, (8, half), f32)
    )
    if fused:
        outputs |= dict(o_fin=(ANY, (blocks + 5, 2, sp, COLS), f32))
    else:
        outputs |= dict(GO=(ANY, (blocks + 5, 2, D, COLS), bf16))
    square, act, total = pltpu.VMEM((D, D), bf16), pltpu.VMEM((T, D), bf16), pltpu.VMEM((T, D), f32)
    small, halves = pltpu.VMEM((8, TILE), f32), pltpu.VMEM((8, half), f32)
    sems = pltpu.SemaphoreType.DMA
    scratch = dict(
        XB=act, OG=act, HN=act, G=act, Y=act, QQ=act, RT=act, RZ=act, T2=act,
        AB=pltpu.VMEM((T, 2 * D), bf16), MM=pltpu.VMEM((T, T), bf16), F1=total, F3=total,
        ST=pltpu.VMEM((T, TILE), f32), WQ=square, WK=square, WV=square, WO=square,
        WU=pltpu.VMEM((2 * D, FH), bf16), WD=pltpu.VMEM((2 * FH, D), bf16),
        SD=pltpu.VMEM((T, 4 * COLS), bf16), SC=pltpu.VMEM((T, TILE), bf16),
        NP=pltpu.VMEM((8, D), f32), NPS=halves, NPR=halves,
        PS=pltpu.VMEM((2, 2, D, COLS), bf16), PR=pltpu.VMEM((2, 2, D, COLS), bf16),
        S=pltpu.VMEM((SLOTS, 2, D, COLS), bf16),
        RX=pltpu.VMEM((SLOTS, 2, D, COLS), bf16) if fused else small,
        FIN=pltpu.VMEM((SLOTS, 2, sp, COLS), f32) if fused else small,
        NG=pltpu.VMEM((4, 8, D), f32), NV=pltpu.VMEM((8, D), f32), NR=pltpu.VMEM((5, 8, half), f32),
        NZS=pltpu.VMEM((nz, 8, half), f32), PBO=pltpu.VMEM((sp, T // 2), f32),
        local_sem=sems((16,)), entry_s=sems((16,)), entry_r=sems((16,)), end_l=sems((2,)), end_s=sems((2,)),
        end_r=sems((2,)), up_l=sems((blocks,)), up_s=sems((blocks,)), up_r=sems((blocks,)),
        down_l=sems((blocks,)), down_s=sems((blocks,)), down_r=sems((blocks,)),
        pair_s=sems((2, 5)), pair_r=sems((2, 5)), ring_s=sems((SLOTS, 2, 6)), ring_r=sems((SLOTS, 2, 6)),
        norm_s=sems((2 + nz,)), norm_r=sems((2 + nz,)), fin_sem=sems((blocks + 5, 2)),
    )
    results = pl.pallas_call(
        functools.partial(
            block_kernel, T, D, FH, R, fused, tuple(inputs) + tuple(outputs) + tuple(scratch)
        ),
        out_shape=tuple(jax.ShapeDtypeStruct(shape, kind) for _, shape, kind in outputs.values()),
        in_specs=[VMEM if name in near else ANY for name in inputs],
        out_specs=tuple(spec for spec, _, _ in outputs.values()),
        scratch_shapes=list(scratch.values()),
        compiler_params=pltpu.CompilerParams(
            collective_id=0, has_side_effects=True, vmem_limit_bytes=63 << 20
        ),
    )(*inputs.values())
    out = SimpleNamespace(**dict(zip(outputs, results)))
    if fused:
        return unpack(T, D, FH, sh, sp, out)
    return gather_parts(T, D, out, pair_bias)


def solution(mesh):
    split, first, second, vector = P("rows", "chan"), P("chan", None), P(None, "chan"), P("chan")
    return jax.shard_map(
        on_device,
        mesh=mesh,
        in_specs=(
            split, P("rows", None), vector, vector, second, second, second, first, vector, vector, second, first,
            P(), split,
        ),
        out_specs=(
            split, split, vector, vector, split, split, split, P("chan", "rows"), vector, vector, split,
            P("chan", "rows"), split,
        ),
        check_vma=False,
    )
```

time: 115 us -> 110 us (0.957)
  Pallas kernels: 114 us -> 109 us
    pallas_call x1, Pallas kernels: 110 us -> 105 us  [on_device(): pl.pallas_call(functools.partial(block_kernel, T, D, FH, R, fused, tuple(...]
where the time goes in v4:
time: 110 us
  Pallas kernels  109 us (99%)
    pallas_call x1, Pallas kernels, on_device(): pl.pallas_call(functools.partial(block_kernel, T, D, FH, R, fused, tuple(...  105 us
    pallas_call x1, Pallas kernels, unpack(): pl.pallas_call(functools.partial(unpack_kernel, sh, blocks, half, count,...  4.53 us

profile of v4, /device:TPU:0, one launch (start us, length us, event | category | flops | bytes accessed | tf_op | source)
XLA Modules:
  0.0 110.2 jit_solution(6872504540416951115)
XLA Ops:
  0.7 104.8 %shard_map.237 = (bf16[2048,384]{1,0:T(8,128)(2,1)}, bf16[2048,384]{1,0:T(8,128)(2,1)}, f32[8,384]{1,0:T(8,128)}, f32[11,2,64,256]{3,2,1,0:T(8,128)}) custom-call(bf16[2048,384]{1,0:T(8,128)(2,1)} %all_refs_0_.1, s32[2,1024]{1,0:T(2,128)} %all_refs_1_.1, f32[384]{0:T(512)} %all_refs_2_.1, f32[384]{0:T(512)} %all_refs_3_.1, bf16[768,384]{1,0:T(8,128)(2,1)} %all_refs_4_.1, ...), custom_call_target="tpu_custom_call" | custom-call | tf_op jit(solution)/shard_map/pallas_call | solution.py:768
  105.5 4.5 %shard_map.238 = (bf16[2048,384]{1,0:T(8,128)(2,1)}, f32[2048,384]{1,0:T(8,128)}, f32[384]{0:T(512)}, f32[384]{0:T(512)}, f32[48,384]{1,0:T(8,128)}, /*index=5*/...) custom-call(bf16[2048,384]{1,0:T(8,128)(2,1)} %get-tuple-element.30., ...), custom_call_target="tpu_custom_call" | custom-call | tf_op jit(solution)/shard_map/pallas_call | solution.py:678

commit v5 on v4

--- a/solution.py
+++ b/solution.py
@@ -14,13 +14,14 @@
 EPSILON = 1e-05
 TILE = 128
 COLS = 256
-SLOTS = 6
+SLOTS = 5
+FINALS = 6
 STEP = 256
 LAGS = (2, 3, 4)
 LATE = (
-    ((-3, 2), (-2, 1)), (), ((-4, 3), (-2, 2), (-1, 1)), (), ((0, 1),), ((-1, 2),), ((-3, 3), (-2, 3)), ((0, 2), (1, 1)),
-    ((2, 1),), ((1, 2),), ((0, 3), (2, 2)), ((3, 1),), ((-1, 3), (4, 1)), ((3, 2),), ((1, 3), (4, 2)),
-    ((2, 3), (3, 3), (4, 3)),
+    ((-3, 2), (-2, 1)), ((-4, 3),), ((-2, 2), (-1, 1)), ((-3, 3),), ((0, 1),), ((-1, 2),), ((-2, 3),), ((0, 2), (1, 1)),
+    ((2, 1),), ((-1, 3), (1, 2)), ((0, 3), (2, 2)), (), ((3, 1), (1, 3)), ((4, 1), (3, 2)), ((2, 3), (4, 2)),
+    ((3, 3), (4, 3)),
 )
 f32 = jnp.float32
 bf16 = jnp.bfloat16
@@ -87,6 +88,11 @@
             src_ref=src, dst_ref=dst, send_sem=send, recv_sem=recv, device_id=device, device_id_type=MESH
         )
 
+    barrier = pltpu.get_barrier_semaphore()
+    greeted = [dev_c] + ([dev_x, dev_y] + dev_z if fused else [])
+    for device in greeted:
+        pl.semaphore_signal(barrier, inc=1, device_id=device, device_id_type=MESH)
+
     my_rows, other_rows = pl.ds(c * T, T), pl.ds(o * T, T)
     h2 = T // 2
     local, cross = [], []
@@ -136,23 +142,20 @@
         pair_rows = pl.ds(pl.multiple_of(r * sp, 8), sp)
         pair_cols = pl.ds(pl.multiple_of(c * (T // 2), TILE), T // 2)
         pbo_at = load(ref.pair_bias.at[pair_rows, pair_cols], ref.PBO)
+
+    NPS[...] = jnp.zeros(NPS.shape, f32)
+    for i, vector in enumerate((ref.gi, ref.si, ref.gm, ref.sm)):
+        NPS[i : i + 1, :] = vector[...].reshape(1, half)
+    norms_cross = remote(NPS, NPR, ref.entry_s.at[15], ref.entry_r.at[15], dev_c)
+    pl.semaphore_wait(barrier, len(greeted))
+    cross[tokens_at].start()
+    norms_cross.start()
+    for at in qkv_at:
+        cross[at].start()
     hidden_weights = [hidden_copies(jnp.int32(i)) for i in range(blocks)]
     for copies in hidden_weights:
         copies[0].start()
         copies[1].start()
-
-    NPS[...] = jnp.zeros(NPS.shape, f32)
-    for i, vector in enumerate((ref.gi, ref.si, ref.gm, ref.sm)):
-        NPS[i : i + 1, :] = vector[...].reshape(1, half)
-    norms_cross = remote(NPS, NPR, ref.entry_s.at[15], ref.entry_r.at[15], dev_c)
-    barrier = pltpu.get_barrier_semaphore()
-    greeted = [dev_c] + ([dev_x, dev_y] + dev_z if fused else [])
-    for device in greeted:
-        pl.semaphore_signal(barrier, inc=1, device_id=device, device_id_type=MESH)
-    pl.semaphore_wait(barrier, len(greeted))
-    norms_cross.start()
-    for at in [tokens_at] + qkv_at:
-        cross[at].start()
 
     def ready(*chosen):
         for at in chosen:
@@ -202,7 +205,7 @@
         ST[rows, 0:1] = inv
         return carry
 
-    lax.fori_loop(0, T // STEP, norm_in, 0)
+    lax.fori_loop(0, T // STEP, norm_in, 0, unroll=2)
     cross[wo_at].start()
     cross[og_at].start()
     for copies in hidden_weights:
@@ -329,7 +332,7 @@
     def fin_copy(ch, part):
         rows, cols = pl.ds(0, ch.height), pl.ds(0, ch.widths[part])
         return pltpu.make_async_copy(
-            FIN.at[lax.rem(ch.k, SLOTS), part, rows, cols], ref.o_fin.at[ch.k, part, rows, cols], ref.fin_sem.at[ch.k, part]
+            FIN.at[lax.rem(ch.k, FINALS), part, rows, cols], ref.o_fin.at[ch.k, part, rows, cols], ref.fin_sem.at[ch.k, part]
         )
 
     def launch(ch):
@@ -366,8 +369,8 @@
                 bias = ref.PBO[:, pl.ds(pl.multiple_of(pair_part[part] * COLS, COLS), COLS)]
                 total = jnp.where(ch.valid[part], total * jnp.exp(bias), 0.0)
             if ch.late:
-                fin_copy(chunk(ch.k - SLOTS), part).wait()
-            FIN[lax.rem(ch.k, SLOTS), part, 0 : ch.height, cols] = total
+                fin_copy(chunk(ch.k - FINALS), part).wait()
+            FIN[lax.rem(ch.k, FINALS), part, 0 : ch.height, cols] = total
             fin_copy(ch, part).start()
 
     def pair_copy(slot):
@@ -423,7 +426,7 @@
         NG[3] += fold_rows(grad)
         return carry
 
-    lax.fori_loop(0, T // STEP, norm_mid_back, 0)
+    lax.fori_loop(0, T // STEP, norm_mid_back, 0, unroll=2)
     blk_local = pltpu.make_async_copy(G.at[:, own_half], ref.o_blk.at[my_rows, :], ref.end_l.at[0])
     blk_cross = remote(G.at[:, other_half], ref.o_blk.at[my_rows, :], ref.end_s.at[0], ref.end_r.at[0], dev_c)
     blk_local.start()
@@ -559,7 +562,7 @@
         NG[1] += fold_rows(grad)
         return carry
 
-    lax.fori_loop(0, T // STEP, norm_in_back, 0)
+    lax.fori_loop(0, T // STEP, norm_in_back, 0, unroll=2)
     tok_local = pltpu.make_async_copy(HN.at[:, own_half], ref.o_tok.at[my_rows, :], ref.end_l.at[1])
     tok_cross = remote(HN.at[:, other_half], ref.o_tok.at[my_rows, :], ref.end_s.at[1], ref.end_r.at[1], dev_c)
     tok_local.start()
@@ -598,7 +601,7 @@
         for j in range(1, nz):
             total = total + NZS[j]
         ref.o_norm[...] = total
-        for k in range(blocks + 5 - SLOTS, blocks + 5):
+        for k in range(blocks + 5 - FINALS, blocks + 5):
             for part in range(2):
                 fin_copy(late_chunk(k - blocks) if k >= blocks else chunk(jnp.int32(k)), part).wait()
     else:
@@ -613,50 +616,61 @@
 def unpack_kernel(sh, blocks, half, count, names, *all_refs):
     ref = SimpleNamespace(**dict(zip(names, all_refs)))
     step = ref.tok_in.shape[0] // count
-    load_b = pltpu.make_async_copy(ref.o_blk, ref.blk, ref.sem.at[0, 0])
-    save_b = pltpu.make_async_copy(ref.blk, ref.r_blk, ref.sem.at[1, 0])
     loads, saves = [], []
-    for i in range(count):
-        rows = slice(i * step, (i + 1) * step)
-        loads.append(pltpu.make_async_copy(ref.o_tok.at[rows, :], ref.tok_in.at[rows, :], ref.sem.at[0, 1 + i]))
-        saves.append(pltpu.make_async_copy(ref.tok_out.at[rows, :], ref.r_tok.at[rows, :], ref.sem.at[1, 1 + i]))
-    load_f = pltpu.make_async_copy(ref.o_fin, ref.fin, ref.sem.at[0, 1 + count])
-    load_n = pltpu.make_async_copy(ref.o_norm, ref.norm, ref.sem.at[1, 1 + count])
-    loads[0].start()
-    load_b.start()
-    for load in loads[1:]:
-        load.start()
-    load_f.start()
-    load_n.start()
-    fin, norm = ref.fin, ref.norm
-    for i in range(count):
-        loads[i].wait()
-        rows = slice(i * step, (i + 1) * step)
-        ref.tok_out[rows, :] = ref.tok_in[rows, :].astype(f32)
-        saves[i].start()
-        if i == 0:
-            load_b.wait()
-            save_b.start()
-    load_n.wait()
-    for i, vector in enumerate((ref.r_gi, ref.r_si, ref.r_gm, ref.r_sm)):
-        vector[...] = norm[i, :]
+
+    def save(src, dst):
+        copy = pltpu.make_async_copy(src, dst, ref.save_sem.at[len(saves)])
+        copy.start()
+        saves.append(copy)
+
+    def load(src, dst):
+        copy = pltpu.make_async_copy(src, dst, ref.load_sem.at[len(loads)])
+        copy.start()
+        loads.append(copy)
+        return copy
+
+    parts = [slice(i * step, (i + 1) * step) for i in range(count)]
+    load_t = [load(ref.o_tok.at[parts[0], :], ref.tok_in.at[parts[0], :])]
+    load_f = load(ref.o_fin, ref.fin)
+    load_n = load(ref.o_norm, ref.norm)
+    load_b = load(ref.o_blk, ref.blk)
+    load_t += [load(ref.o_tok.at[rows, :], ref.tok_in.at[rows, :]) for rows in parts[1:]]
+
+    def widen(i):
+        load_t[i].wait()
+        ref.tok_out[parts[i], :] = ref.tok_in[parts[i], :].astype(f32)
+        save(ref.tok_out.at[parts[i], :], ref.r_tok.at[parts[i], :])
+
+    widen(0)
     load_f.wait()
+    fin = ref.fin
     for k in range(blocks):
         cols = slice(k * COLS, (k + 1) * COLS)
-        ref.r_up[:, cols] = fin[k, 0, 0:sh, :]
-        ref.r_dn[:, cols] = fin[k, 1, 0:sh, :]
+        ref.up[:, cols] = fin[k, 0, 0:sh, :]
+        ref.dn[:, cols] = fin[k, 1, 0:sh, :]
+    save(ref.up, ref.r_up)
+    save(ref.dn, ref.r_dn)
     low, high = fin[blocks + 2, 0], fin[blocks + 2, 1]
     first = lax.axis_index("chan") == 0
-    ref.r_pair[:, 0:COLS] = jnp.where(first, low, high)
-    ref.r_pair[:, COLS : 2 * COLS] = jnp.where(first, high, low)
-    for late, target in ((0, ref.r_wo), (1, ref.r_q), (3, ref.r_k), (4, ref.r_v)):
+    ref.pair[:, 0:COLS] = jnp.where(first, low, high)
+    ref.pair[:, COLS : 2 * COLS] = jnp.where(first, high, low)
+    save(ref.pair, ref.r_pair)
+    for i, (late, target) in enumerate(((0, ref.r_wo), (1, ref.r_q), (3, ref.r_k), (4, ref.r_v))):
         at = 0
-        for part, width in enumerate(widths_of(half, late if late < 2 else late - 1)):
-            target[:, at : at + width] = fin[blocks + late, part, 0:sh, 0:width]
+        for part, width in enumerate(widths_of(half, i)):
+            ref.square[i, :, at : at + width] = fin[blocks + late, part, 0:sh, 0:width]
             at += width
-    for save in saves:
-        save.wait()
-    save_b.wait()
+        save(ref.square.at[i], target)
+    load_n.wait()
+    for i, (vector, target) in enumerate(((ref.gi, ref.r_gi), (ref.si, ref.r_si), (ref.gm, ref.r_gm), (ref.sm, ref.r_sm))):
+        vector[...] = ref.norm[i, :]
+        save(vector, target)
+    load_b.wait()
+    save(ref.blk, ref.r_blk)
+    for i in range(1, count):
+        widen(i)
+    for copy in saves:
+        copy.wait()
 
 
 def unpack(T, D, FH, sh, sp, out):
@@ -664,22 +678,24 @@
     blocks = FH // COLS
     count = 4
     inputs = dict(o_blk=out.o_blk, o_tok=out.o_tok, o_norm=out.o_norm, o_fin=out.o_fin)
-    vector, square, wide = (VMEM, (half,), f32), (VMEM, (sh, half), f32), (VMEM, (sh, FH), f32)
+    vector, square, wide = ((half,), f32), ((sh, half), f32), ((sh, FH), f32)
     results = dict(
-        r_blk=(ANY, (2 * T, half), bf16), r_tok=(ANY, (2 * T, half), f32), r_gi=vector, r_si=vector, r_q=square,
-        r_k=square, r_v=square, r_wo=square, r_gm=vector, r_sm=vector, r_up=wide, r_dn=wide,
-        r_pair=(VMEM, (sp, T // 2), f32),
-    )
+        r_blk=((2 * T, half), bf16), r_tok=((2 * T, half), f32), r_gi=vector, r_si=vector, r_q=square, r_k=square,
+        r_v=square, r_wo=square, r_gm=vector, r_sm=vector, r_up=wide, r_dn=wide, r_pair=((sp, T // 2), f32),
+    )
+    held = pltpu.VMEM((half,), f32)
     scratch = dict(
         blk=pltpu.VMEM((2 * T, half), bf16), tok_in=pltpu.VMEM((2 * T, half), bf16),
-        tok_out=pltpu.VMEM((2 * T, half), f32), sem=pltpu.SemaphoreType.DMA((2, 2 + count)),
-        fin=pltpu.VMEM(out.o_fin.shape, f32), norm=pltpu.VMEM((8, half), f32),
+        tok_out=pltpu.VMEM((2 * T, half), f32), fin=pltpu.VMEM(out.o_fin.shape, f32),
+        norm=pltpu.VMEM((8, half), f32), up=pltpu.VMEM((sh, FH), f32), dn=pltpu.VMEM((sh, FH), f32),
+        pair=pltpu.VMEM((sp, T // 2), f32), square=pltpu.VMEM((4, sh, half), f32), gi=held, si=held, gm=held, sm=held,
+        load_sem=pltpu.SemaphoreType.DMA((3 + count,)), save_sem=pltpu.SemaphoreType.DMA((len(results) - 1 + count,)),
     )
     values = pl.pallas_call(
         functools.partial(unpack_kernel, sh, blocks, half, count, tuple(inputs) + tuple(results) + tuple(scratch)),
-        out_shape=tuple(jax.ShapeDtypeStruct(shape, kind) for _, shape, kind in results.values()),
+        out_shape=tuple(jax.ShapeDtypeStruct(shape, kind) for shape, kind in results.values()),
         in_specs=[ANY] * len(inputs),
-        out_specs=tuple(spec for spec, _, _ in results.values()),
+        out_specs=tuple(ANY for _ in results),
         scratch_shapes=list(scratch.values()),
         compiler_params=pltpu.CompilerParams(vmem_limit_bytes=63 << 20),
     )(*inputs.values())
@@ -756,7 +772,7 @@
         PS=pltpu.VMEM((2, 2, D, COLS), bf16), PR=pltpu.VMEM((2, 2, D, COLS), bf16),
         S=pltpu.VMEM((SLOTS, 2, D, COLS), bf16),
         RX=pltpu.VMEM((SLOTS, 2, D, COLS), bf16) if fused else small,
-        FIN=pltpu.VMEM((SLOTS, 2, sp, COLS), f32) if fused else small,
+        FIN=pltpu.VMEM((FINALS, 2, sp, COLS), f32) if fused else small,
         NG=pltpu.VMEM((4, 8, D), f32), NV=pltpu.VMEM((8, D), f32), NR=pltpu.VMEM((5, 8, half), f32),
         NZS=pltpu.VMEM((nz, 8, half), f32), PBO=pltpu.VMEM((sp, T // 2), f32),
         local_sem=sems((16,)), entry_s=sems((16,)), entry_r=sems((16,)), end_l=sems((2,)), end_s=sems((2,)),

time: 110 us -> 110 us (level)
  no operation moved by 1% of the time
where the time goes in v5:
time: 110 us
  Pallas kernels  109 us (99%)
    pallas_call x1, Pallas kernels, on_device(): pl.pallas_call(functools.partial(block_kernel, T, D, FH, R, fused, tuple(...  105 us
    pallas_call x1, Pallas kernels, unpack(): pl.pallas_call(functools.partial(unpack_kernel, sh, blocks, half, count,...  4.12 us

profile of v5, /device:TPU:0, one launch (start us, length us, event | category | flops | bytes accessed | tf_op | source)
XLA Modules:
  0.0 110.0 jit_solution(359526513120594136)
XLA Ops:
  0.7 105.0 %shard_map.237 = (bf16[2048,384]{1,0:T(8,128)(2,1)}, bf16[2048,384]{1,0:T(8,128)(2,1)}, f32[8,384]{1,0:T(8,128)}, f32[11,2,64,256]{3,2,1,0:T(8,128)}) custom-call(bf16[2048,384]{1,0:T(8,128)(2,1)} %all_refs_0_.1, s32[2,1024]{1,0:T(2,128)} %all_refs_1_.1, f32[384]{0:T(512)} %all_refs_2_.1, f32[384]{0:T(512)} %all_refs_3_.1, bf16[768,384]{1,0:T(8,128)(2,1)} %all_refs_4_.1, ...), custom_call_target="tpu_custom_call" | custom-call | tf_op jit(solution)/shard_map/pallas_call | solution.py:784
  105.7 4.1 %shard_map.238 = (bf16[2048,384]{1,0:T(8,128)(2,1)}, f32[2048,384]{1,0:T(8,128)}, f32[384]{0:T(512)}, f32[384]{0:T(512)}, f32[48,384]{1,0:T(8,128)}, /*index=5*/...) custom-call(bf16[2048,384]{1,0:T(8,128)(2,1)} %get-tuple-element.30., ...), custom_call_target="tpu_custom_call" | custom-call | tf_op jit(solution)/shard_map/pallas_call | solution.py:694

commit v6 on v5

--- a/solution.py
+++ b/solution.py
@@ -633,7 +633,8 @@
     load_t = [load(ref.o_tok.at[parts[0], :], ref.tok_in.at[parts[0], :])]
     load_f = load(ref.o_fin, ref.fin)
     load_n = load(ref.o_norm, ref.norm)
-    load_b = load(ref.o_blk, ref.blk)
+    rows_b = [slice(i * step * count // 2, (i + 1) * step * count // 2) for i in range(2)]
+    load_b = [load(ref.o_blk.at[rows, :], ref.blk.at[rows, :]) for rows in rows_b]
     load_t += [load(ref.o_tok.at[rows, :], ref.tok_in.at[rows, :]) for rows in parts[1:]]
 
     def widen(i):
@@ -665,8 +666,9 @@
     for i, (vector, target) in enumerate(((ref.gi, ref.r_gi), (ref.si, ref.r_si), (ref.gm, ref.r_gm), (ref.sm, ref.r_sm))):
         vector[...] = ref.norm[i, :]
         save(vector, target)
-    load_b.wait()
-    save(ref.blk, ref.r_blk)
+    for copy, rows in zip(load_b, rows_b):
+        copy.wait()
+        save(ref.blk.at[rows, :], ref.r_blk.at[rows, :])
     for i in range(1, count):
         widen(i)
     for copy in saves:
@@ -676,7 +678,7 @@
 def unpack(T, D, FH, sh, sp, out):
     half = D // 2
     blocks = FH // COLS
-    count = 4
+    count = 8
     inputs = dict(o_blk=out.o_blk, o_tok=out.o_tok, o_norm=out.o_norm, o_fin=out.o_fin)
     vector, square, wide = ((half,), f32), ((sh, half), f32), ((sh, FH), f32)
     results = dict(
@@ -689,7 +691,7 @@
         tok_out=pltpu.VMEM((2 * T, half), f32), fin=pltpu.VMEM(out.o_fin.shape, f32),
         norm=pltpu.VMEM((8, half), f32), up=pltpu.VMEM((sh, FH), f32), dn=pltpu.VMEM((sh, FH), f32),
         pair=pltpu.VMEM((sp, T // 2), f32), square=pltpu.VMEM((4, sh, half), f32), gi=held, si=held, gm=held, sm=held,
-        load_sem=pltpu.SemaphoreType.DMA((3 + count,)), save_sem=pltpu.SemaphoreType.DMA((len(results) - 1 + count,)),
+        load_sem=pltpu.SemaphoreType.DMA((4 + count,)), save_sem=pltpu.SemaphoreType.DMA((len(results) + count,)),
     )
     values = pl.pallas_call(
         functools.partial(unpack_kernel, sh, blocks, half, count, tuple(inputs) + tuple(results) + tuple(scratch)),

time: 110 us -> 110 us (level)
  no operation moved by 1% of the time
where the time goes in v6:
time: 110 us
  Pallas kernels  109 us (99%)
    pallas_call x1, Pallas kernels, on_device(): pl.pallas_call(functools.partial(block_kernel, T, D, FH, R, fused, tuple(...  105 us
    pallas_call x1, Pallas kernels, unpack(): pl.pallas_call(functools.partial(unpack_kernel, sh, blocks, half, count,...  4.16 us

profile of v6, /device:TPU:0, one launch (start us, length us, event | category | flops | bytes accessed | tf_op | source)
XLA Modules:
  0.0 110.0 jit_solution(3612212194260146)
XLA Ops:
  0.7 105.0 %shard_map.237 = (bf16[2048,384]{1,0:T(8,128)(2,1)}, bf16[2048,384]{1,0:T(8,128)(2,1)}, f32[8,384]{1,0:T(8,128)}, f32[11,2,64,256]{3,2,1,0:T(8,128)}) custom-call(bf16[2048,384]{1,0:T(8,128)(2,1)} %all_refs_0_.1, s32[2,1024]{1,0:T(2,128)} %all_refs_1_.1, f32[384]{0:T(512)} %all_refs_2_.1, f32[384]{0:T(512)} %all_refs_3_.1, bf16[768,384]{1,0:T(8,128)(2,1)} %all_refs_4_.1, ...), custom_call_target="tpu_custom_call" | custom-call | tf_op jit(solution)/shard_map/pallas_call | solution.py:786
  105.7 4.2 %shard_map.238 = (bf16[2048,384]{1,0:T(8,128)(2,1)}, f32[2048,384]{1,0:T(8,128)}, f32[384]{0:T(512)}, f32[384]{0:T(512)}, f32[48,384]{1,0:T(8,128)}, /*index=5*/...) custom-call(bf16[2048,384]{1,0:T(8,128)(2,1)} %get-tuple-element.30., ...), custom_call_target="tpu_custom_call" | custom-call | tf_op jit(solution)/shard_map/pallas_call | solution.py:696
